TPU v7x, 32 devices: a whole 2x2x4 slice. The times are simulated.
32 devices in a mesh: grp: 8 (over y, x, core), seq: 4 (over z).
Axes of the slice: x: 2, y: 2, z: 4, core: 2. Of those that a mesh axis runs over, the one named last changes fastest.
Arguments:
- inputs: bfloat16 [8, 2, 1536, 768], P('grp', None, 'seq'), may hold values from -6 to 6
- clip_frames: int32 [8, 2], P('grp'), may hold values from 96 to 384, as said below
- cotangent: bfloat16 [8, 2, 1536, 768], P('grp', None, 'seq'), may hold values from -6 to 6
- w_query: bfloat16 [768, 768], P(('grp', 'seq')), may hold values from -0.3125 to 0.3125
- w_key: bfloat16 [768, 768], P(('grp', 'seq')), may hold values from -0.3125 to 0.3125
- w_value: bfloat16 [768, 768], P(('grp', 'seq')), may hold values from -0.21875 to 0.21875
- w_out: bfloat16 [768, 768], P(('grp', 'seq')), may hold values from -0.875 to 0.875
- w_up: bfloat16 [768, 3072], P(('grp', 'seq')), may hold values from -0.21875 to 0.21875
- w_down: bfloat16 [3072, 768], P(('grp', 'seq')), may hold values from -0.15625 to 0.15625
- b_query: bfloat16 [768], P(('grp', 'seq')), may hold values from -3 to 3
- b_value: bfloat16 [768], P(('grp', 'seq')), may hold values from -1.796875 to 1.796875
- b_out: bfloat16 [768], P(('grp', 'seq')), may hold values from -3 to 3
- b_up: bfloat16 [3072], P(('grp', 'seq')), may hold values from -3 to 3
- b_down: bfloat16 [768], P(('grp', 'seq')), may hold values from -3 to 3
- gain_one: bfloat16 [768], P(('grp', 'seq')), may hold values from 0.5 to 1.5
- shift_one: bfloat16 [768], P(('grp', 'seq')), may hold values from -1.796875 to 1.796875
- gain_two: bfloat16 [768], P(('grp', 'seq')), may hold values from 0.5 to 1.5
- shift_two: bfloat16 [768], P(('grp', 'seq')), may hold values from -1.796875 to 1.796875
Outputs:
- layer_out: bfloat16 [8, 2, 1536, 768], P('grp', None, 'seq')
- grad_inputs: bfloat16 [8, 2, 1536, 768], P('grp', None, 'seq')
- grad_w_query: float32 [768, 768], P(('grp', 'seq'))
- grad_w_key: float32 [768, 768], P(('grp', 'seq'))
- grad_w_value: float32 [768, 768], P(('grp', 'seq'))
- grad_w_out: float32 [768, 768], P(('grp', 'seq'))
- grad_w_up: float32 [768, 3072], P(('grp', 'seq'))
- grad_w_down: float32 [3072, 768], P(('grp', 'seq'))
- grad_b_query: float32 [768], P(('grp', 'seq'))
- grad_b_value: float32 [768], P(('grp', 'seq'))
- grad_b_out: float32 [768], P(('grp', 'seq'))
- grad_b_up: float32 [3072], P(('grp', 'seq'))
- grad_b_down: float32 [768], P(('grp', 'seq'))
- grad_gain_one: float32 [768], P(('grp', 'seq'))
- grad_shift_one: float32 [768], P(('grp', 'seq'))
- grad_gain_two: float32 [768], P(('grp', 'seq'))
- grad_shift_two: float32 [768], P(('grp', 'seq'))
Inputs may be any that keep to these rules, and one draw needn't show every extreme that they name: Every slice of clip slot (g, s) holds clip_frames[g, s] live frames at its start; in every draw one slot has exactly 384 and another exactly 96.
All inputs are finite; a program needn't handle non-finite values.
Results may differ from a plain program's by a relative error of at most 0.015.
Values may be sent and summed in bfloat16 or wider, within the bound.
A program may use at most 192 MiB of HBM per device.

v0:
```python
import jax
import jax.numpy as jnp
from jax import lax
from jax.sharding import PartitionSpec as P

HEAD = 64


epsilon = 1e-05
score_scale = 0.125
sqrt_half = 0.7071067811865476
inv_root_tau = 0.3989422804014327


def standardize(token_rows):
    row_mean = jnp.mean(token_rows, -1, keepdims=True)
    centred = token_rows - row_mean
    inverse = lax.rsqrt(jnp.mean(centred * centred, -1, keepdims=True) + epsilon)
    return (centred * inverse, inverse)


def norm_back(grad_out, normed, inverse, gain_vec):
    scaled = grad_out * gain_vec
    grad_rows = inverse * (
        scaled
        - jnp.mean(scaled, -1, keepdims=True)
        - normed * jnp.mean(scaled * normed, -1, keepdims=True)
    )
    return (grad_rows, jnp.sum(grad_out * normed, 0), jnp.sum(grad_out, 0))


def gelu_slope(hidden):
    return (
        0.5 * (1.0 + lax.erf(hidden * sqrt_half))
        + hidden * jnp.exp(-0.5 * hidden * hidden) * inv_root_tau
    )


def split_heads(block, pair_count):
    slot_count, length, width = block.shape
    return block.reshape(slot_count, length, pair_count, 2, HEAD).transpose(2, 0, 1, 3, 4)


def merge_heads(block):
    pair_count, slot_count, length, twin_heads, head_size = block.shape
    return block.transpose(1, 2, 0, 3, 4).reshape(
        slot_count, length, pair_count * twin_heads * head_size
    )


def body(
    inputs,
    clip_frames,
    cotangent,
    w_query,
    w_key,
    w_value,
    w_out,
    w_up,
    w_down,
    b_query,
    b_value,
    b_out,
    b_up,
    b_down,
    gain_one,
    shift_one,
    gain_two,
    shift_two,
):
    shards = (
        w_query,
        w_key,
        w_value,
        w_out,
        w_up,
        w_down,
        b_query,
        b_value,
        b_out,
        b_up,
        b_down,
        gain_one,
        shift_one,
        gain_two,
        shift_two,
    )
    (
        wq_full,
        wk_full,
        wv_full,
        wo_full,
        up_full,
        down_full,
        bq_full,
        bv_full,
        bo_full,
        bu_full,
        bd_full,
        gain_first,
        shift_first,
        gain_second,
        shift_second,
    ) = (
        lax.all_gather(shards[0], ("grp", "seq"), axis=0, tiled=True),
        lax.all_gather(shards[1], ("grp", "seq"), axis=0, tiled=True),
        lax.all_gather(shards[2], ("grp", "seq"), axis=0, tiled=True),
        lax.all_gather(shards[3], ("grp", "seq"), axis=0, tiled=True),
        lax.all_gather(shards[4], ("grp", "seq"), axis=0, tiled=True),
        lax.all_gather(shards[5], ("grp", "seq"), axis=0, tiled=True),
        lax.all_gather(shards[6], ("grp", "seq"), axis=0, tiled=True),
        lax.all_gather(shards[7], ("grp", "seq"), axis=0, tiled=True),
        lax.all_gather(shards[8], ("grp", "seq"), axis=0, tiled=True),
        lax.all_gather(shards[9], ("grp", "seq"), axis=0, tiled=True),
        lax.all_gather(shards[10], ("grp", "seq"), axis=0, tiled=True),
        lax.all_gather(shards[11], ("grp", "seq"), axis=0, tiled=True),
        lax.all_gather(shards[12], ("grp", "seq"), axis=0, tiled=True),
        lax.all_gather(shards[13], ("grp", "seq"), axis=0, tiled=True),
        lax.all_gather(shards[14], ("grp", "seq"), axis=0, tiled=True),
    )
    slot_count, slice_len, width = (inputs.shape[1], inputs.shape[2], inputs.shape[3])
    row_count = slot_count * slice_len
    pair_count = width // (2 * HEAD)
    token_rows = inputs[0].astype(jnp.float32).reshape(row_count, width)
    normed_one, inverse_one = standardize(token_rows)
    first_in = (
        normed_one * gain_first.astype(jnp.float32) + shift_first.astype(jnp.float32)
    ).astype(jnp.bfloat16)
    queries = (
        jnp.dot(first_in, wq_full, preferred_element_type=jnp.float32) + bq_full.astype(jnp.float32)
    ).astype(jnp.bfloat16)
    key_local = jnp.dot(first_in, wk_full, preferred_element_type=jnp.float32).astype(jnp.bfloat16)
    value_local = (
        jnp.dot(first_in, wv_full, preferred_element_type=jnp.float32) + bv_full.astype(jnp.float32)
    ).astype(jnp.bfloat16)
    key_all, value_all = (
        lax.all_gather(key_local.reshape(slot_count, slice_len, width), "seq", axis=1, tiled=True),
        lax.all_gather(
            value_local.reshape(slot_count, slice_len, width), "seq", axis=1, tiled=True
        ),
    )
    clip_len = key_all.shape[1]
    offsets = jnp.arange(clip_len, dtype=jnp.int32) % slice_len
    live_keys = offsets[None, :] < clip_frames[0][:, None]
    query_heads = split_heads(queries.reshape(slot_count, slice_len, width), pair_count)
    key_heads = split_heads(key_all, pair_count)
    value_heads = split_heads(value_all, pair_count)

    def masked_scores(query_block, key_block, live_mask):
        scores = (
            jnp.einsum(
                "cqhd,ckhd->chqk", query_block, key_block, preferred_element_type=jnp.float32
            )
            * score_scale
        )
        return jnp.where(live_mask[:, None, None, :], scores, -1e30)

    def attend(pieces):
        query_block, key_block, value_block = pieces
        scores = masked_scores(query_block, key_block, live_keys)
        row_max = jnp.max(scores, -1, keepdims=True)
        exponent = jnp.exp(scores - row_max)
        row_sum = jnp.sum(exponent, -1, keepdims=True)
        weights = (exponent / row_sum).astype(jnp.bfloat16)
        mixed_block = jnp.einsum(
            "chqk,ckhd->cqhd", weights, value_block, preferred_element_type=jnp.float32
        )
        return (mixed_block, (row_max + jnp.log(row_sum))[..., 0])

    mixed_heads, logsum = lax.map(attend, (query_heads, key_heads, value_heads))
    mixed_low = merge_heads(mixed_heads).reshape(row_count, width).astype(jnp.bfloat16)
    branch = jnp.dot(mixed_low, wo_full, preferred_element_type=jnp.float32) + bo_full.astype(
        jnp.float32
    )
    middle = token_rows + branch
    normed_two, inverse_two = standardize(middle)
    second_in = (
        normed_two * gain_second.astype(jnp.float32) + shift_second.astype(jnp.float32)
    ).astype(jnp.bfloat16)
    hidden = jnp.dot(second_in, up_full, preferred_element_type=jnp.float32) + bu_full.astype(
        jnp.float32
    )
    active_low = jax.nn.gelu(hidden, approximate=False).astype(jnp.bfloat16)
    result = (
        middle
        + jnp.dot(active_low, down_full, preferred_element_type=jnp.float32)
        + bd_full.astype(jnp.float32)
    )
    layer_out = result.astype(jnp.bfloat16).reshape(inputs.shape)
    (
        wq_full,
        wk_full,
        wv_full,
        wo_full,
        up_full,
        down_full,
        bq_full,
        bv_full,
        bo_full,
        bu_full,
        bd_full,
        gain_first,
        shift_first,
        gain_second,
        shift_second,
    ) = (
        lax.all_gather(shards[0], ("grp", "seq"), axis=0, tiled=True),
        lax.all_gather(shards[1], ("grp", "seq"), axis=0, tiled=True),
        lax.all_gather(shards[2], ("grp", "seq"), axis=0, tiled=True),
        lax.all_gather(shards[3], ("grp", "seq"), axis=0, tiled=True),
        lax.all_gather(shards[4], ("grp", "seq"), axis=0, tiled=True),
        lax.all_gather(shards[5], ("grp", "seq"), axis=0, tiled=True),
        lax.all_gather(shards[6], ("grp", "seq"), axis=0, tiled=True),
        lax.all_gather(shards[7], ("grp", "seq"), axis=0, tiled=True),
        lax.all_gather(shards[8], ("grp", "seq"), axis=0, tiled=True),
        lax.all_gather(shards[9], ("grp", "seq"), axis=0, tiled=True),
        lax.all_gather(shards[10], ("grp", "seq"), axis=0, tiled=True),
        lax.all_gather(shards[11], ("grp", "seq"), axis=0, tiled=True),
        lax.all_gather(shards[12], ("grp", "seq"), axis=0, tiled=True),
        lax.all_gather(shards[13], ("grp", "seq"), axis=0, tiled=True),
        lax.all_gather(shards[14], ("grp", "seq"), axis=0, tiled=True),
    )
    grad_top = cotangent[0].reshape(row_count, width)
    grad_rows = grad_top.astype(jnp.float32)
    grad_down = jnp.dot(active_low.T, grad_top, preferred_element_type=jnp.float32)
    gbias_down = jnp.sum(grad_rows, 0)
    grad_active = jnp.dot(grad_top, down_full.T, preferred_element_type=jnp.float32)
    grad_hidden = (grad_active * gelu_slope(hidden)).astype(jnp.bfloat16)
    grad_up = jnp.dot(second_in.T, grad_hidden, preferred_element_type=jnp.float32)
    gbias_up = jnp.sum(grad_hidden.astype(jnp.float32), 0)
    grad_second = jnp.dot(grad_hidden, up_full.T, preferred_element_type=jnp.float32)
    grad_norm_two, grad_gain_two, grad_shift_two = norm_back(
        grad_second, normed_two, inverse_two, gain_second.astype(jnp.float32)
    )
    grad_middle = grad_rows + grad_norm_two
    grad_branch = grad_middle.astype(jnp.bfloat16)
    grad_out = jnp.dot(mixed_low.T, grad_branch, preferred_element_type=jnp.float32)
    gbias_out = jnp.sum(grad_branch.astype(jnp.float32), 0)
    grad_mixed = jnp.dot(grad_branch, wo_full.T, preferred_element_type=jnp.float32).astype(
        jnp.bfloat16
    )
    mixed_grad_heads = split_heads(grad_mixed.reshape(slot_count, slice_len, width), pair_count)

    def score_grads(query_block, key_block, value_block, grad_block, logsum_block, live_mask):
        scores = masked_scores(query_block, key_block, live_mask)
        weights = jnp.exp(scores - logsum_block[..., None])
        grad_weights = jnp.einsum(
            "cqhd,ckhd->chqk", grad_block, value_block, preferred_element_type=jnp.float32
        )
        return (weights, grad_weights)

    def attend_back(pieces):
        query_block, key_block, value_block, grad_block, logsum_block = pieces
        weights, grad_weights = score_grads(
            query_block, key_block, value_block, grad_block, logsum_block, live_keys
        )
        inner_sum = jnp.sum(weights * grad_weights, -1, keepdims=True)
        grad_scores = (weights * (grad_weights - inner_sum)).astype(jnp.bfloat16)
        grad_query_block = (
            jnp.einsum(
                "chqk,ckhd->cqhd", grad_scores, key_block, preferred_element_type=jnp.float32
            )
            * score_scale
        )
        grad_key_block = (
            jnp.einsum(
                "chqk,cqhd->ckhd", grad_scores, query_block, preferred_element_type=jnp.float32
            )
            * score_scale
        )
        grad_value_block = jnp.einsum(
            "chqk,cqhd->ckhd",
            weights.astype(jnp.bfloat16),
            grad_block,
            preferred_element_type=jnp.float32,
        )
        return (grad_query_block, grad_key_block, grad_value_block)

    gq_heads, gk_heads, gv_heads = lax.map(
        attend_back, (query_heads, key_heads, value_heads, mixed_grad_heads, logsum)
    )
    key_grads, value_grads = (
        lax.psum_scatter(
            merge_heads(gk_heads).astype(jnp.bfloat16), "seq", scatter_dimension=1, tiled=True
        ).astype(jnp.float32),
        lax.psum_scatter(
            merge_heads(gv_heads).astype(jnp.bfloat16), "seq", scatter_dimension=1, tiled=True
        ).astype(jnp.float32),
    )
    grad_key = key_grads.reshape(row_count, width).astype(jnp.bfloat16)
    grad_value = value_grads.reshape(row_count, width).astype(jnp.bfloat16)
    grad_query = merge_heads(gq_heads).reshape(row_count, width).astype(jnp.bfloat16)
    gw_query = jnp.dot(first_in.T, grad_query, preferred_element_type=jnp.float32)
    gw_key = jnp.dot(first_in.T, grad_key, preferred_element_type=jnp.float32)
    gw_value = jnp.dot(first_in.T, grad_value, preferred_element_type=jnp.float32)
    gbias_query = jnp.sum(grad_query.astype(jnp.float32), 0)
    gbias_value = jnp.sum(grad_value.astype(jnp.float32), 0)
    grad_first = jnp.dot(grad_query, wq_full.T, preferred_element_type=jnp.float32)
    grad_first = grad_first + jnp.dot(grad_key, wk_full.T, preferred_element_type=jnp.float32)
    grad_first = grad_first + jnp.dot(grad_value, wv_full.T, preferred_element_type=jnp.float32)
    grad_norm_one, grad_gain_one, grad_shift_one = norm_back(
        grad_first, normed_one, inverse_one, gain_first.astype(jnp.float32)
    )
    grad_inputs = (grad_middle + grad_norm_one).astype(jnp.bfloat16).reshape(inputs.shape)
    summed_all = (
        lax.psum_scatter(gw_query, ("grp", "seq"), scatter_dimension=0, tiled=True),
        lax.psum_scatter(gw_key, ("grp", "seq"), scatter_dimension=0, tiled=True),
        lax.psum_scatter(gw_value, ("grp", "seq"), scatter_dimension=0, tiled=True),
        lax.psum_scatter(grad_out, ("grp", "seq"), scatter_dimension=0, tiled=True),
        lax.psum_scatter(grad_up, ("grp", "seq"), scatter_dimension=0, tiled=True),
        lax.psum_scatter(grad_down, ("grp", "seq"), scatter_dimension=0, tiled=True),
        lax.psum_scatter(gbias_query, ("grp", "seq"), scatter_dimension=0, tiled=True),
        lax.psum_scatter(gbias_value, ("grp", "seq"), scatter_dimension=0, tiled=True),
        lax.psum_scatter(gbias_out, ("grp", "seq"), scatter_dimension=0, tiled=True),
        lax.psum_scatter(gbias_up, ("grp", "seq"), scatter_dimension=0, tiled=True),
        lax.psum_scatter(gbias_down, ("grp", "seq"), scatter_dimension=0, tiled=True),
        lax.psum_scatter(grad_gain_one, ("grp", "seq"), scatter_dimension=0, tiled=True),
        lax.psum_scatter(grad_shift_one, ("grp", "seq"), scatter_dimension=0, tiled=True),
        lax.psum_scatter(grad_gain_two, ("grp", "seq"), scatter_dimension=0, tiled=True),
        lax.psum_scatter(grad_shift_two, ("grp", "seq"), scatter_dimension=0, tiled=True),
    )
    return (
        layer_out,
        grad_inputs,
        summed_all[0],
        summed_all[1],
        summed_all[2],
        summed_all[3],
        summed_all[4],
        summed_all[5],
        summed_all[6],
        summed_all[7],
        summed_all[8],
        summed_all[9],
        summed_all[10],
        summed_all[11],
        summed_all[12],
        summed_all[13],
        summed_all[14],
    )


def solution(mesh):
    return jax.shard_map(
        body,
        mesh=mesh,
        in_specs=(
            P("grp", None, "seq", None),
            P("grp", None),
            P("grp", None, "seq", None),
            P(("grp", "seq"), None),
            P(("grp", "seq"), None),
            P(("grp", "seq"), None),
            P(("grp", "seq"), None),
            P(("grp", "seq"), None),
            P(("grp", "seq"), None),
            P(("grp", "seq")),
            P(("grp", "seq")),
            P(("grp", "seq")),
            P(("grp", "seq")),
            P(("grp", "seq")),
            P(("grp", "seq")),
            P(("grp", "seq")),
            P(("grp", "seq")),
            P(("grp", "seq")),
        ),
        out_specs=(
            P("grp", None, "seq", None),
            P("grp", None, "seq", None),
            P(("grp", "seq"), None),
            P(("grp", "seq"), None),
            P(("grp", "seq"), None),
            P(("grp", "seq"), None),
            P(("grp", "seq"), None),
            P(("grp", "seq"), None),
            P(("grp", "seq")),
            P(("grp", "seq")),
            P(("grp", "seq")),
            P(("grp", "seq")),
            P(("grp", "seq")),
            P(("grp", "seq")),
            P(("grp", "seq")),
            P(("grp", "seq")),
            P(("grp", "seq")),
        ),
        check_vma=False,
    )
```

profile of v0, /device:TPU:9, one launch (start us, length us, event | category | flops | bytes accessed | tf_op | source)
XLA Modules:
  0.0 1667.0 jit_solution(11885890830249403467)
XLA Ops:
  17.0 41.4 %all-reduce.19 = (bf16[768]{0:T(1024)(128)(2,1)S(1)}, bf16[768]{0:T(1024)(128)(2,1)S(1)}, bf16[768]{0:T(1024)(128)(2,1)S(1)}, bf16[768]{0:T(1024)(128)(2,1)}, bf...) all-reduce(bf16[768]{0:T(1024)(128)(2,1)S(1)} %dynamic-update-slice, ...), channel_id=1, replica_groups=mesh['grp'=8,'seq'=4] {'grp','seq'}, use_global_device_ids=true, to_apply=%add.1 | all-reduce | flops 9216 | bytes 36864
  69.6 52.1 %all-gather.15.cloned.1.call-done = bf16[768,768]{1,0:T(8,128)(2,1)} async-done(((bf16[24,768]{1,0:T(8,128)(2,1)}), bf16[768,768]{1,0:T(8,128)(2,1)}) %all-gather.15.cloned.1.call-update) | async-done | bytes 1179664 | tf_op jit(solution)/shard_map/all_gather | solution.py:106
  132.9 44.6 %all-gather.13.cloned.1.call-done = bf16[768,768]{1,0:T(8,128)(2,1)} async-done(((bf16[24,768]{1,0:T(8,128)(2,1)}), bf16[768,768]{1,0:T(8,128)(2,1)}) %all-gather.13.cloned.1.call-update) | async-done | bytes 1179664 | tf_op jit(solution)/shard_map/all_gather | solution.py:105
  181.1 84.8 %all-gather.11.cloned.1.call-done = bf16[2,1536,768]{1,2,0:T(8,128)(2,1)} async-done(((bf16[2,384,768]{1,2,0:T(8,128)(2,1)}), bf16[2,1536,768]{1,2,0:T(8,128)(2,1)}) %all-gather.11.cloned.1.call-update) | async-done | bytes 4718608 | tf_op jit(solution)/shard_map/all_gather | solution.py:138
  265.9 5.0 copy.72
  270.9 84.9 %all-gather.17.cloned.1.call-done = bf16[2,1536,768]{1,2,0:T(8,128)(2,1)} async-done(((bf16[2,384,768]{1,2,0:T(8,128)(2,1)}), bf16[2,1536,768]{1,2,0:T(8,128)(2,1)}) %all-gather.17.cloned.1.call-update) | async-done | bytes 4718608 | tf_op jit(solution)/shard_map/all_gather | solution.py:137
  355.8 5.0 copy.74
  360.9 54.2 %while.28 = (s32[]{:T(128)}, bf16[6,2,384,2,64]{2,4,3,1,0:T(8,128)(2,1)S(1)}, f32[6,2,2,384]{3,2,1,0:T(2,128)}, bf16[6,2,1536,2,64]{2,4,3,1,0:T(8,128)(2,1)}, bf...) while((s32[]{:T(128)}, ...), condition=%wide.region_5.6_spmd.clone, body=%wide.region_2.5_spmd.clone.sunk | while | flops 632292864 | bytes 30550128 | solution.py:170
  365.8 3.5 fusion.148
  374.8 3.5 fusion.148
  383.9 3.6 fusion.148
  401.9 3.5 fusion.148
  410.9 3.5 fusion.148
  421.5 58.3 %all-gather.21.cloned.1.call-done = bf16[768,3072]{1,0:T(8,128)(2,1)} async-done(((bf16[24,3072]{1,0:T(8,128)(2,1)}), bf16[768,3072]{1,0:T(8,128)(2,1)}) %all-gather.21.cloned.1.call-update) | async-done | bytes 4718608 | tf_op jit(solution)/shard_map/all_gather | solution.py:109
  479.8 28.1 %fusion.49 = (bf16[768,3072]{1,0:T(8,128)(2,1)}, f32[768,3072]{1,0:T(8,128)}) fusion(f32[3072]{0:T(1024)} %convert_element_type.182, bf16[768,3072]{1,0:T(8,128)(2,1)} %all-gather.21.cloned.1.call-done, f32[768,768]{1,0:T(8,128)S(1)} %get-tuple-element.288, f32[768]{0:T(1024)} %convert_element_type.180, f32[768]{0:T(1024)S(1)} %convert_element_type.179, ...), kind=kOutput, calls=%fused_computation.59 | convolution fusion | flops 3782541312 | bytes 21258240 | tf_op jit(solution)/shard_map/dot_general | solution.py:180
  507.9 37.1 %all-gather.23.cloned.1.call-done = bf16[3072,768]{1,0:T(8,128)(2,1)} async-done(((bf16[96,768]{1,0:T(8,128)(2,1)}), bf16[3072,768]{1,0:T(8,128)(2,1)}) %all-gather.23.cloned.1.call-update) | async-done | bytes 4718608 | tf_op jit(solution)/shard_map/all_gather | solution.py:110
  545.0 10.2 convert_reduce_fusion
  555.2 4.9 multiply_reduce_fusion.1
  569.4 201.9 %while.29 = (s32[]{:T(128)}, bf16[6,2,384,2,64]{2,4,3,1,0:T(8,128)(2,1)}, bf16[6,2,1536,2,64]{2,4,3,0,1:T(8,128)(2,1)}, bf16[6,2,1536,2,64]{2,4,3,0,1:T(8,128)(2...) while((s32[]{:T(128)}, ...), condition=%wide.region_12.13_spmd.clone, body=%wide.region_10.12_spmd.clone.sunk | while | flops 1531676160 | bytes 153400592 | solution.py:279
  573.8 8.7 multiply_reduce_fusion.7
  582.5 9.4 multiply_convert_fusion.2
  591.9 4.9 fusion.156
  596.8 4.3 fusion.157
  607.5 8.7 multiply_reduce_fusion.7
  616.2 9.4 multiply_convert_fusion.2
  625.6 4.9 fusion.156
  630.5 4.3 fusion.157
  641.2 8.7 multiply_reduce_fusion.7
  649.9 9.4 multiply_convert_fusion.2
  659.2 4.9 fusion.156
  664.2 4.3 fusion.157
  674.8 8.7 multiply_reduce_fusion.7
  683.5 9.4 multiply_convert_fusion.2
  692.8 4.9 fusion.156
  697.8 4.3 fusion.157
  708.4 8.7 multiply_reduce_fusion.7
  717.1 9.4 multiply_convert_fusion.2
  726.5 4.9 fusion.156
  731.4 4.3 fusion.157
  742.1 8.7 multiply_reduce_fusion.7
  750.7 9.4 multiply_convert_fusion.2
  760.1 4.9 fusion.156
  765.0 4.3 fusion.157
  771.2 12.5 copy.86
  783.7 5.5 copy.116
  789.3 12.6 copy.88
  801.9 5.5 copy.117
  815.1 4.6 fusion.85
  819.8 52.9 %reduce-scatter.25.cloned.1.call-done = bf16[384,1536]{1,0:T(8,128)(2,1)} async-done(((bf16[1536,1536]{1,0:T(8,128)(2,1)}), bf16[384,1536]{1,0:T(8,128)(2,1)}) %reduce-scatter.25.cloned.1.call-update) | async-done | bytes 1179664
  872.7 3.7 reshape.274
  881.4 79.2 %reduce-scatter.27.cloned.1.call-done = bf16[384,1536]{1,0:T(8,128)(2,1)} async-done(((bf16[1536,1536]{1,0:T(8,128)(2,1)}), bf16[384,1536]{1,0:T(8,128)(2,1)}) %reduce-scatter.27.cloned.1.call-update) | async-done | bytes 1179664
  960.6 3.7 reshape.276
  970.1 9.0 fusion.88
  979.4 10.3 fusion.96
  994.7 4.3 fusion.91
  999.0 8.7 add_convert_fusion
  1007.7 3.7 copy.89
  1015.0 3.8 fusion.81
  1018.7 41.7 %all-reduce.18 = (f32[768]{0:T(1024)}, f32[768]{0:T(1024)}, f32[768]{0:T(1024)}, f32[3072]{0:T(1024)}, f32[768]{0:T(1024)}, /*index=5*/f32[768]{0:T(1024)}, f32[768]{0:T(1024)}, f32[768]{0:T(1024)}, f32[768]{0:T(1024)}) all-reduce(f32[768]{0:T(1024)} %reduce_sum.182, ...), channel_id=10, replica_groups=mesh['grp'=8,'seq'=4] {'grp','seq'}, use_global_device_ids=true, to_apply=%region_24.25.clone | all-reduce | flops 9216 | bytes 73728
  1076.2 92.7 %reduce-scatter.19.cloned.1.call-done = f32[24,768]{1,0:T(8,128)} async-done(((f32[768,768]{1,0:T(8,128)}), f32[24,768]{1,0:T(8,128)}) %reduce-scatter.19.cloned.1.call-update) | async-done | bytes 73744 | tf_op jit(solution)/shard_map/reduce_scatter | solution.py:309
  1169.0 103.9 %reduce-scatter.15.cloned.1.call-done = f32[24,768]{1,0:T(8,128)} async-done(((f32[768,768]{1,0:T(8,128)}), f32[24,768]{1,0:T(8,128)}) %reduce-scatter.15.cloned.1.call-update) | async-done | bytes 73744 | tf_op jit(solution)/shard_map/reduce_scatter | solution.py:307
  1272.9 104.6 %reduce-scatter.17.cloned.1.call-done = f32[24,768]{1,0:T(8,128)} async-done(((f32[768,768]{1,0:T(8,128)}), f32[24,768]{1,0:T(8,128)}) %reduce-scatter.17.cloned.1.call-update) | async-done | bytes 73744 | tf_op jit(solution)/shard_map/reduce_scatter | solution.py:308
  1377.5 140.4 %reduce-scatter.21.cloned.1.call-done = f32[24,3072]{1,0:T(8,128)} async-done(((f32[768,3072]{1,0:T(8,128)}), f32[24,3072]{1,0:T(8,128)}) %reduce-scatter.21.cloned.1.call-update) | async-done | bytes 294928 | tf_op jit(solution)/shard_map/reduce_scatter | solution.py:310
  1517.9 142.1 %reduce-scatter.23.cloned.1.call-done = f32[96,768]{1,0:T(8,128)} async-done(((f32[3072,768]{1,0:T(8,128)}), f32[96,768]{1,0:T(8,128)}) %reduce-scatter.23.cloned.1.call-update) | async-done | bytes 294928 | tf_op jit(solution)/shard_map/reduce_scatter | solution.py:311
  (286 shorter events, 168.8 us)
Async XLA Ops:
  7.2 55.1 %copy-start.2 = (bf16[1,2,384,768]{3,2,1,0:T(8,128)(2,1)S(1)}, bf16[1,2,384,768]{3,2,1,0:T(8,128)(2,1)}, u32[]{:S(2)}) copy-start(bf16[1,2,384,768]{3,2,1,0:T(8,128)(2,1)} %param.22) | copy-start | bytes 3538948
  7.2 58.6 %all-gather.9.cloned.1.call-start = ((), (), s32[]{:S(2)}) async-start(), calls=%async_computation.8 | async-start | bytes 1216512 | tf_op jit(solution)/shard_map/all_gather | solution.py:107
  7.9 113.7 %all-gather.15.cloned.1.call-start = ((), (), s32[]{:S(2)}) async-start(), calls=%async_computation.11 | async-start | bytes 1216512 | tf_op jit(solution)/shard_map/all_gather | solution.py:106
  8.7 168.9 %all-gather.13.cloned.1.call-start = ((), (), s32[]{:S(2)}) async-start(), calls=%async_computation.10 | async-start | bytes 1216512 | tf_op jit(solution)/shard_map/all_gather | solution.py:105
  9.4 256.4 %all-gather.11.cloned.1.call-start = ((), (), s32[]{:S(2)}) async-start(), calls=%async_computation.9 | async-start | bytes 5898240 | tf_op jit(solution)/shard_map/all_gather | solution.py:138
  58.4 4.4 copy-start.32
  58.4 4.4 copy-start.21
  59.9 1.8 copy-start.26
  60.0 2.9 copy-start.28
  69.6 286.2 %all-gather.17.cloned.1.call-start = ((), (), s32[]{:S(2)}) async-start(), calls=%async_computation.12 | async-start | bytes 5898240 | tf_op jit(solution)/shard_map/all_gather | solution.py:137
  125.5 292.1 %all-gather.19.cloned.1.call-start = ((), (), s32[]{:S(2)}) async-start(), calls=%async_computation.13 | async-start | bytes 1216512 | tf_op jit(solution)/shard_map/all_gather | solution.py:108
  126.0 353.7 %all-gather.21.cloned.1.call-start = ((), (), s32[]{:S(2)}) async-start(), calls=%async_computation.14 | async-start | bytes 4866048 | tf_op jit(solution)/shard_map/all_gather | solution.py:109
  126.8 418.2 %all-gather.23.cloned.1.call-start = ((), (), s32[]{:S(2)}) async-start(), calls=%async_computation.15 | async-start | bytes 4866048 | tf_op jit(solution)/shard_map/all_gather | solution.py:110
  127.5 745.1 %reduce-scatter.25.cloned.1.call-start = ((), (), s32[]{:S(2)}) async-start(), calls=%async_computation.22 | async-start | bytes 5898240
  355.8 5.1 copy-start.24
  415.1 2.5 copy-start.4
  415.1 2.5 copy-start.35
  421.5 123.5 %copy-start.8 = (bf16[1,2,384,768]{3,2,1,0:T(8,128)(2,1)S(1)}, bf16[1,2,384,768]{3,2,1,0:T(8,128)(2,1)}, u32[]{:S(2)}) copy-start(bf16[1,2,384,768]{3,2,1,0:T(8,128)(2,1)} %param.24) | copy-start | bytes 3538948
  545.0 10.2 copy-start.18
  545.0 10.2 copy-start.37
  555.2 4.9 copy-start.9
  560.1 3.1 copy-start.39
  561.8 1.5 copy-start.6
  570.4 3.3 copy-start.25
  573.0 9.5 copy-start.1
  591.9 9.2 copy-start
  604.1 3.3 copy-start.25
  606.7 9.5 copy-start.1
  625.6 9.2 copy-start
  637.8 3.3 copy-start.25
  640.3 9.5 copy-start.1
  659.2 9.2 copy-start
  671.4 3.3 copy-start.25
  673.9 9.5 copy-start.1
  692.8 9.2 copy-start
  705.0 3.3 copy-start.25
  707.6 9.5 copy-start.1
  726.5 9.2 copy-start
  738.6 3.3 copy-start.25
  741.2 9.5 copy-start.1
  760.1 9.3 copy-start
  789.2 171.4 %reduce-scatter.27.cloned.1.call-start = ((), (), s32[]{:S(2)}) async-start(), calls=%async_computation.23 | async-start | bytes 5898240
  807.4 1.3 copy-start.3
  807.4 1.3 copy-start.22
  807.4 1.3 copy-start.27
  807.4 268.8 %reduce-scatter.13.cloned.1.call-start = ((), (), s32[]{:S(2)}) async-start(), calls=%async_computation.16 | async-start | bytes 2433024 | tf_op jit(solution)/shard_map/reduce_scatter | solution.py:306
  808.7 1.3 copy-start.5
  809.9 1.5 copy-start.15
  815.0 353.9 %reduce-scatter.19.cloned.1.call-start = ((), (), s32[]{:S(2)}) async-start(), calls=%async_computation.19 | async-start | bytes 2433024 | tf_op jit(solution)/shard_map/reduce_scatter | solution.py:309
  819.8 453.1 %reduce-scatter.15.cloned.1.call-start = ((), (), s32[]{:S(2)}) async-start(), calls=%async_computation.17 | async-start | bytes 2433024 | tf_op jit(solution)/shard_map/reduce_scatter | solution.py:307
  876.3 2.5 copy-start.16
  881.4 496.1 %reduce-scatter.17.cloned.1.call-start = ((), (), s32[]{:S(2)}) async-start(), calls=%async_computation.18 | async-start | bytes 2433024 | tf_op jit(solution)/shard_map/reduce_scatter | solution.py:308
  964.3 2.5 copy-start.17
  969.4 548.5 %reduce-scatter.21.cloned.1.call-start = ((), (), s32[]{:S(2)}) async-start(), calls=%async_computation.20 | async-start | bytes 9732096 | tf_op jit(solution)/shard_map/reduce_scatter | solution.py:310
  979.1 681.0 %reduce-scatter.23.cloned.1.call-start = ((), (), s32[]{:S(2)}) async-start(), calls=%async_computation.21 | async-start | bytes 9732096 | tf_op jit(solution)/shard_map/reduce_scatter | solution.py:311
  1007.7 4.5 copy-start.12
  1012.2 2.6 copy-start.14
  1012.2 2.6 copy-start.23
  1012.2 2.6 copy-start.29
  1012.2 2.6 copy-start.31
  1012.2 2.6 copy-start.38
  1012.2 2.7 copy-start.40
  1015.0 3.8 copy-start.34
  1015.0 58.2 %copy-start.7 = (f32[768,768]{1,0:T(8,128)S(1)}, f32[768,768]{1,0:T(8,128)}, u32[]{:S(2)}) copy-start(f32[768,768]{1,0:T(8,128)} %copy-done.6) | copy-start | bytes 7077892
  (8 other events, 6.8 us)
Sparse Core Ops, SparseCore 0:
  10.8 54.8 all-gather.8
  68.6 53.0 all-gather.14
  124.5 53.0 all-gather.12
  179.6 86.2 all-gather.10
  267.9 87.8 all-gather.16
  358.4 54.6 all-gather.18
  415.9 63.7 all-gather.20
  482.6 62.3 all-gather.22
  789.3 83.2 reduce-scatter.24
  874.8 85.7 reduce-scatter.26
  966.5 97.7 reduce-scatter.12
  1070.9 98.0 reduce-scatter.18
  1174.8 98.0 reduce-scatter.14
  1279.5 98.0 reduce-scatter.16
  1383.8 134.0 reduce-scatter.20
  1525.3 134.7 reduce-scatter.22
where the time goes:
time: 1680 us; the launch traced here: 1670 us
  waiting for transfers between devices  1080 us (64%)
  matrix products  278 us (17%)
  local copies, waits for them, and re-layouts  110 us (7%)
  other arithmetic  95 us (6%)
  blocking collectives  83.1 us (5%)
    reduce_scatter x1, waiting for transfers between devices, body(): lax.psum_scatter(grad_down, ('grp', 'seq'), scatter_dimension=0, tiled=True)  142 us
    reduce_scatter x1, waiting for transfers between devices, body(): lax.psum_scatter(grad_up, ('grp', 'seq'), scatter_dimension=0, tiled=True)  140 us
    unnamed x18, waiting for transfers between devices  136 us
    reduce_scatter x1, waiting for transfers between devices, body(): lax.psum_scatter(gw_value, ('grp', 'seq'), scatter_dimension=0, tiled=True)  105 us
    reduce_scatter x1, waiting for transfers between devices, body(): lax.psum_scatter(gw_key, ('grp', 'seq'), scatter_dimension=0, tiled=True)  104 us
    reduce_scatter x1, waiting for transfers between devices, body(): lax.psum_scatter(grad_out, ('grp', 'seq'), scatter_dimension=0, tiled=True)  92.7 us
    unnamed x115, local copies, waits for them, and re-layouts  85.2 us
    all_gather x1, waiting for transfers between devices, body(): lax.all_gather(key_local.reshape(slot_count, slice_len, width), 'seq', ax...  84.9 us
  transfers between devices with their start and end apart: 16, of which 14 were waited for; matrix products, arithmetic and copies ran while one was open for 14% of the time, Pallas kernels for 0%

commit v1 on v0

v1 whole, which is shorter than its diff:
```python
import functools

import jax
import jax.numpy as jnp
from jax import lax
from jax.experimental import pallas as pl
from jax.experimental.pallas import tpu as pltpu
from jax.sharding import PartitionSpec as P

HEAD = 64


epsilon = 1e-05
score_scale = 0.125
sqrt_half = 0.7071067811865476
inv_root_tau = 0.3989422804014327


def standardize(token_rows):
    row_mean = jnp.mean(token_rows, -1, keepdims=True)
    centred = token_rows - row_mean
    inverse = lax.rsqrt(jnp.mean(centred * centred, -1, keepdims=True) + epsilon)
    return (centred * inverse, inverse)


def norm_back(grad_out, normed, inverse, gain_vec):
    scaled = grad_out * gain_vec
    grad_rows = inverse * (
        scaled
        - jnp.mean(scaled, -1, keepdims=True)
        - normed * jnp.mean(scaled * normed, -1, keepdims=True)
    )
    return (grad_rows, jnp.sum(grad_out * normed, 0), jnp.sum(grad_out, 0))


def gelu_slope(hidden):
    return (
        0.5 * (1.0 + lax.erf(hidden * sqrt_half))
        + hidden * jnp.exp(-0.5 * hidden * hidden) * inv_root_tau
    )


PAIR = 2 * HEAD
Q_BLOCK = 256
NT = (((1,), (1,)), ((), ()))
f32 = jnp.float32
bf16 = jnp.bfloat16


def head_mask(head, width):
    lane = lax.broadcasted_iota(jnp.int32, (1, width), 1)
    chosen = lane < HEAD if head == 0 else lane >= HEAD
    return chosen.astype(f32).astype(bf16)


def nt(left, right):
    return lax.dot_general(left, right, NT, preferred_element_type=f32)


def attend_kernel(q_ref, ko_ref, kx_ref, vo_ref, vx_ref, bias_ref, out_ref, lse_ref):
    queries = q_ref[...] * jnp.asarray(score_scale, bf16)
    keys = jnp.concatenate([ko_ref[...], kx_ref[...]], 0)
    values_t = jnp.concatenate([vo_ref[...], vx_ref[...]], 0).T
    bias = jnp.concatenate([bias_ref[...]] * 2, 0)
    mixed = []
    for head in range(2):
        scores = nt(keys, queries * head_mask(head, PAIR)) + bias
        row_max = jnp.max(scores, 0, keepdims=True)
        exponent = jnp.exp(scores - row_max)
        row_sum = jnp.sum(exponent, 0, keepdims=True)
        part = jnp.dot(
            values_t[head * HEAD : (head + 1) * HEAD],
            exponent.astype(bf16),
            preferred_element_type=f32,
        )
        mixed.append(part * (1.0 / row_sum))
        lse_ref[0, head : head + 1, :] = row_max + jnp.log(row_sum)
    out_ref[...] = jnp.concatenate(mixed, 0).T.astype(bf16)


def attend_back_kernel(
    q_ref, ko_ref, kx_ref, vo_ref, vx_ref, bias_ref, out_ref, grad_ref, lse_ref,
    dq_ref, dko_ref, dvo_ref, dkx_ref, dvx_ref, dk_acc, dv_acc,
):
    step = pl.program_id(1)
    queries = q_ref[...] * jnp.asarray(score_scale, bf16)
    grads = grad_ref[...]
    keys = jnp.concatenate([ko_ref[...], kx_ref[...]], 0)
    keys_t = keys.T
    values = jnp.concatenate([vo_ref[...], vx_ref[...]], 0)
    bias = jnp.concatenate([bias_ref[...]] * 2, 0)
    inner = (grads.astype(f32) * out_ref[...].astype(f32)).T
    grad_queries = []
    grad_keys = grad_values = None
    for head in range(2):
        mask = head_mask(head, PAIR)
        rows = slice(head * HEAD, (head + 1) * HEAD)
        query_head, grad_head = queries * mask, grads * mask
        scores = nt(keys, query_head) + bias
        weights = jnp.exp(scores - lse_ref[0, head : head + 1, :])
        inner_sum = jnp.sum(inner[rows], 0, keepdims=True)
        grad_scores = (weights * (nt(values, grad_head) - inner_sum)).astype(bf16)
        value_part = jnp.dot(weights.astype(bf16), grad_head, preferred_element_type=f32)
        key_part = jnp.dot(grad_scores, query_head, preferred_element_type=f32)
        grad_values = value_part if head == 0 else grad_values + value_part
        grad_keys = key_part if head == 0 else grad_keys + key_part
        grad_queries.append(jnp.dot(keys_t[rows], grad_scores, preferred_element_type=f32))
    dq_ref[...] = (jnp.concatenate(grad_queries, 0).T * score_scale).astype(bf16)

    @pl.when(step == 0)
    def _():
        dk_acc[...] = grad_keys
        dv_acc[...] = grad_values

    @pl.when(step > 0)
    def _():
        dk_acc[...] += grad_keys
        dv_acc[...] += grad_values

    @pl.when(step == pl.num_programs(1) - 1)
    def _():
        half = dko_ref.shape[0]
        dko_ref[...] = dk_acc[:half].astype(bf16)
        dkx_ref[...] = dk_acc[half:].astype(bf16)
        dvo_ref[...] = dv_acc[:half].astype(bf16)
        dvx_ref[...] = dv_acc[half:].astype(bf16)


def attention_specs(rows, pairs, first):
    whole = lambda shift: pl.BlockSpec((rows, PAIR), lambda p, i: (0, p + first + shift))
    return [
        pl.BlockSpec((Q_BLOCK, PAIR), lambda p, i: (i, p + first)),
        whole(pairs),
        whole(0),
        whole(2 * pairs),
        whole(pairs),
        pl.BlockSpec((rows, Q_BLOCK), lambda p, i: (0, 0)),
    ]


def attend(qkv, kv_other, bias):
    rows, width = qkv.shape[0], qkv.shape[1] // 3
    pairs = width // PAIR
    return pl.pallas_call(
        attend_kernel,
        grid=(pairs, rows // Q_BLOCK),
        in_specs=attention_specs(rows, pairs, 0),
        out_specs=[
            pl.BlockSpec((Q_BLOCK, PAIR), lambda p, i: (i, p)),
            pl.BlockSpec((1, 8, Q_BLOCK), lambda p, i: (p, 0, i)),
        ],
        out_shape=[
            jax.ShapeDtypeStruct((rows, width), bf16),
            jax.ShapeDtypeStruct((pairs, 8, rows), f32),
        ],
        compiler_params=pltpu.CompilerParams(vmem_limit_bytes=40 * 2**20),
        cost_estimate=pl.CostEstimate(
            flops=32 * rows * rows * width,
            bytes_accessed=14 * rows * width,
            transcendentals=2 * rows * rows * width // HEAD,
        ),
    )(qkv, qkv, kv_other, qkv, kv_other, bias)


def attend_back(qkv, kv_other, bias, mixed, grads, lse, first, count):
    rows, width = mixed.shape
    pairs = width // PAIR
    block = lambda: pl.BlockSpec((Q_BLOCK, PAIR), lambda p, i: (i, p + first))
    return pl.pallas_call(
        attend_back_kernel,
        grid=(count, rows // Q_BLOCK),
        in_specs=attention_specs(rows, pairs, first)
        + [block(), block(), pl.BlockSpec((1, 8, Q_BLOCK), lambda p, i: (p + first, 0, i))],
        out_specs=[pl.BlockSpec((Q_BLOCK, PAIR), lambda p, i: (i, p))]
        + [pl.BlockSpec((rows, PAIR), lambda p, i: (0, p))] * 4,
        out_shape=[jax.ShapeDtypeStruct((rows, count * PAIR), bf16)] * 5,
        scratch_shapes=[pltpu.VMEM((2 * rows, PAIR), f32)] * 2,
        compiler_params=pltpu.CompilerParams(vmem_limit_bytes=40 * 2**20),
        cost_estimate=pl.CostEstimate(
            flops=80 * rows * rows * count * PAIR,
            bytes_accessed=24 * rows * count * PAIR,
            transcendentals=4 * rows * rows * count,
        ),
    )(qkv, qkv, kv_other, qkv, kv_other, bias, mixed, grads, lse)


def pick(block, index, axis):
    return lax.dynamic_index_in_dim(block, index, axis, keepdims=False)


def scatter_sum(total, grp_size, seq_size):
    grp, seq = lax.axis_index("grp"), lax.axis_index("seq")
    unit, columns = total.shape[0] // grp_size, total.shape[1]
    left, bit = grp_size, 1
    while left > 1:
        left //= 2
        total = total.reshape(left, 2, unit, columns)
        mine = (grp // bit) % 2
        arrived = lax.ppermute(
            pick(total, 1 - mine, 1).astype(bf16), "grp", [(i, i ^ bit) for i in range(grp_size)]
        )
        total = pick(total, mine, 1) + arrived.astype(f32)
        bit *= 2
    total = total.reshape(seq_size, unit // seq_size, columns)
    result = pick(total, seq, 0)
    for offset in range(1, seq_size):
        arrived = lax.ppermute(
            pick(total, (seq + offset) % seq_size, 0).astype(bf16),
            "seq",
            [(i, (i + offset) % seq_size) for i in range(seq_size)],
        )
        result = result + arrived.astype(f32)
    return result


def body(
    grp_size, seq_size,
    inputs, clip_frames, cotangent,
    w_query, w_key, w_value, w_out, w_up, w_down,
    b_query, b_value, b_out, b_up, b_down,
    gain_one, shift_one, gain_two, shift_two,
):
    axes = ("grp", "seq")
    slot_count, slice_len, width = inputs.shape[1:]
    hidden_width = w_up.shape[1]
    depth = w_query.shape[0]
    spread = hidden_width // width
    row_count = slot_count * slice_len
    grp, seq = lax.axis_index("grp"), lax.axis_index("seq")

    def route(flip):
        moves = []
        for g in range(grp_size):
            for s in range(seq_size):
                slot = (s + flip) % 2
                target = (g // 2 * 2 + s // 2) * seq_size + g % 2 * 2 + slot
                moves.append((g * seq_size + s, target))
        return moves

    routes = (route(0), route(1))
    back_routes = tuple([(b, a) for a, b in moves] for moves in routes)
    swap = [(g, g ^ 1) for g in range(grp_size)]
    parity = seq % 2

    def to_clip(block):
        return jnp.concatenate(
            [
                lax.ppermute(pick(block[0], (parity + flip) % 2, 0), axes, routes[flip])
                for flip in range(2)
            ],
            0,
        )

    def from_clip(rows):
        same, other = (
            lax.ppermute(rows[flip * slice_len : (flip + 1) * slice_len], axes, back_routes[flip])
            for flip in range(2)
        )
        even = parity == 0
        return jnp.stack([jnp.where(even, same, other), jnp.where(even, other, same)])[None]

    vectors = jnp.stack(
        [b_query, b_value, b_out, b_down, gain_one, shift_one, gain_two, shift_two], 1
    )
    vectors = jnp.concatenate([vectors, b_up.reshape(depth, spread)], 1)
    vectors = jnp.pad(vectors, ((0, 0), (0, 128 - vectors.shape[1])))
    early = lax.all_gather(
        jnp.concatenate([w_query, w_key, w_value, vectors], 1), axes, axis=0, tiled=True
    )
    late_shard = jnp.concatenate([w_out, w_up, w_down.reshape(depth, hidden_width)], 1)
    early, late_shard = lax.optimization_barrier((early, late_shard))
    late = lax.all_gather(late_shard, axes, axis=0, tiled=True)
    w_qkv = early[:, : 3 * width]
    columns = early[:, 3 * width :].astype(f32).T
    bq, bv, bo, bd, gain_first, shift_first, gain_second, shift_second = (
        columns[i] for i in range(8)
    )
    bu = columns[8 : 8 + spread].T.reshape(hidden_width)
    wo_full = late[:, :width]
    up_full = late[:, width : width + hidden_width]
    down_full = late[:, width + hidden_width :].reshape(hidden_width, width)

    frames_other = lax.ppermute(clip_frames, "grp", swap)
    frames = jnp.where(seq // 2 == grp % 2, clip_frames, frames_other)[0]
    frame_count = jnp.where(parity == 0, frames[0], frames[1])
    offsets = jnp.arange(row_count, dtype=jnp.int32) % slice_len
    bias = jnp.broadcast_to(
        jnp.where(offsets < frame_count, 0.0, -1e30).astype(f32)[:, None], (row_count, Q_BLOCK)
    )

    token_rows = to_clip(inputs).astype(f32)
    grad_top = to_clip(cotangent)
    normed_one, inverse_one = standardize(token_rows)
    first_in = (normed_one * gain_first + shift_first).astype(bf16)
    b_qkv = jnp.concatenate([bq, jnp.zeros_like(bq), bv])
    qkv = (jnp.dot(first_in, w_qkv, preferred_element_type=f32) + b_qkv).astype(bf16)
    kv_other = lax.ppermute(qkv[:, width:], "grp", swap)
    mixed_low, lse = attend(qkv, kv_other, bias)
    middle = token_rows + jnp.dot(mixed_low, wo_full, preferred_element_type=f32) + bo
    normed_two, inverse_two = standardize(middle)
    second_in = (normed_two * gain_second + shift_second).astype(bf16)
    hidden = jnp.dot(second_in, up_full, preferred_element_type=f32) + bu
    active_low = jax.nn.gelu(hidden, approximate=False).astype(bf16)
    result = middle + jnp.dot(active_low, down_full, preferred_element_type=f32) + bd
    layer_out = from_clip(result.astype(bf16))

    grad_rows = grad_top.astype(f32)
    grad_down = jnp.dot(active_low.T, grad_top, preferred_element_type=f32)
    gbias_down = jnp.sum(grad_rows, 0)
    grad_active = jnp.dot(grad_top, down_full.T, preferred_element_type=f32)
    grad_hidden = (grad_active * gelu_slope(hidden)).astype(bf16)
    grad_up = jnp.dot(second_in.T, grad_hidden, preferred_element_type=f32)
    gbias_up = jnp.sum(grad_hidden.astype(f32), 0)
    grad_second = jnp.dot(grad_hidden, up_full.T, preferred_element_type=f32)
    grad_norm_two, grad_gain_two, grad_shift_two = norm_back(
        grad_second, normed_two, inverse_two, gain_second
    )
    grad_middle = grad_rows + grad_norm_two
    grad_branch = grad_middle.astype(bf16)
    grad_out = jnp.dot(mixed_low.T, grad_branch, preferred_element_type=f32)
    gbias_out = jnp.sum(grad_branch.astype(f32), 0)
    grad_mixed = jnp.dot(grad_branch, wo_full.T, preferred_element_type=f32).astype(bf16)

    out_down = scatter_sum(grad_down, grp_size, seq_size)
    out_up = scatter_sum(grad_up, grp_size, seq_size)
    out_out = scatter_sum(grad_out, grp_size, seq_size)

    pairs = width // PAIR
    count = 1
    grad_q, grad_k, grad_v = [], [], []
    for start in range(0, pairs, count):
        dq, dko, dvo, dkx, dvx = attend_back(
            qkv, kv_other, bias, mixed_low, grad_mixed, lse, start, count
        )
        grad_q.append(dq)
        for own, other, kept in ((dko, dkx, grad_k), (dvo, dvx, grad_v)):
            arrived = lax.ppermute(other, "grp", swap)
            kept.append((own.astype(f32) + arrived.astype(f32)).astype(bf16))
    grad_qkv = jnp.concatenate(grad_q + grad_k + grad_v, 1)
    gw_qkv = jnp.dot(first_in.T, grad_qkv, preferred_element_type=f32)
    gbias_qkv = jnp.sum(grad_qkv.astype(f32), 0)
    grad_first = lax.dot_general(grad_qkv, w_qkv, NT, preferred_element_type=f32)
    grad_norm_one, grad_gain_one, grad_shift_one = norm_back(
        grad_first, normed_one, inverse_one, gain_first
    )
    grad_inputs = from_clip((grad_middle + grad_norm_one).astype(bf16))
    sums = jnp.stack(
        [
            gbias_qkv[:width], gbias_qkv[2 * width :], gbias_out, gbias_down,
            grad_gain_one, grad_shift_one, grad_gain_two, grad_shift_two,
        ]
    )
    sums = jnp.concatenate([sums, gbias_up.reshape(width, spread).T], 0)
    sums = jnp.pad(sums, ((0, 128 - sums.shape[0]), (0, 0))).T
    out_qkv = scatter_sum(gw_qkv, grp_size, seq_size)
    out_sums = scatter_sum(sums, grp_size, seq_size)
    return (
        layer_out,
        grad_inputs,
        out_qkv[:, :width],
        out_qkv[:, width : 2 * width],
        out_qkv[:, 2 * width :],
        out_out,
        out_up,
        out_down,
        out_sums[:, 0],
        out_sums[:, 1],
        out_sums[:, 2],
        out_sums[:, 8 : 8 + spread].reshape(-1),
        out_sums[:, 3],
        out_sums[:, 4],
        out_sums[:, 5],
        out_sums[:, 6],
        out_sums[:, 7],
    )


def solution(mesh):
    return jax.shard_map(
        functools.partial(body, mesh.shape["grp"], mesh.shape["seq"]),
        mesh=mesh,
        in_specs=(
            P("grp", None, "seq", None),
            P("grp", None),
            P("grp", None, "seq", None),
            P(("grp", "seq"), None),
            P(("grp", "seq"), None),
            P(("grp", "seq"), None),
            P(("grp", "seq"), None),
            P(("grp", "seq"), None),
            P(("grp", "seq"), None),
            P(("grp", "seq")),
            P(("grp", "seq")),
            P(("grp", "seq")),
            P(("grp", "seq")),
            P(("grp", "seq")),
            P(("grp", "seq")),
            P(("grp", "seq")),
            P(("grp", "seq")),
            P(("grp", "seq")),
        ),
        out_specs=(
            P("grp", None, "seq", None),
            P("grp", None, "seq", None),
            P(("grp", "seq"), None),
            P(("grp", "seq"), None),
            P(("grp", "seq"), None),
            P(("grp", "seq"), None),
            P(("grp", "seq"), None),
            P(("grp", "seq"), None),
            P(("grp", "seq")),
            P(("grp", "seq")),
            P(("grp", "seq")),
            P(("grp", "seq")),
            P(("grp", "seq")),
            P(("grp", "seq")),
            P(("grp", "seq")),
            P(("grp", "seq")),
            P(("grp", "seq")),
        ),
        check_vma=False,
    )
```

time: 1680 us -> 624 us (0.37)
  waiting for transfers between devices: 1080 us -> 240 us
  matrix products: 278 us -> 86.7 us
  Pallas kernels: 0 us -> 95.2 us
  blocking collectives: 83.1 us -> 0 us
  other arithmetic: 95 us -> 37.6 us
  starting transfers between devices: 1.32 us -> 47.3 us
  local copies, waits for them, and re-layouts: 110 us -> 92.3 us
    reduce_scatter x6 -> x0, waiting for transfers between devices: 584 us -> none  [the longest x1 142 us: body(): lax.psum_scatter(grad_down, ('grp', 'seq'), scatter_dimension=0, tiled=True)]
    all_gather x8 -> x2, waiting for transfers between devices: 365 us -> 59.4 us  [the longest x1 59.4 us: body(): lax.all_gather(jnp.concatenate([w_query, w_key, w_value, vectors], 1), ax...]
    dot_general x60 -> x12, matrix products: 278 us -> 86.7 us  [the longest x1 28.6 us: body(): hidden = jnp.dot(second_in, up_full, preferred_element_type=f32) + bu]
    ppermute x0 -> x52, waiting for transfers between devices: none -> 181 us  [the longest x4 83.3 us: to_clip(): lax.ppermute(pick(block[0], (parity + flip) % 2, 0), axes, routes[flip])]
    unnamed x18 -> x2, waiting for transfers between devices: 136 us -> 0.03 us
    pallas_call x0 -> x7, Pallas kernels: none -> 95.2 us  [the longest x6 53.9 us: attend_back(): pl.pallas_call(attend_back_kernel, grid=(count, rows // Q_BLOCK), in_spec...]
    unnamed x2 -> x0, blocking collectives: 83.1 us -> none
    convert_element_type x18 -> x1, other arithmetic: 66.1 us -> 0.76 us  [body(): grad_inputs = from_clip((grad_middle + grad_norm_one).astype(bf16))]
  transfers between devices with their start and end apart: 16 -> 54, of which waited for: 14 -> 21; matrix products, arithmetic and copies ran while one was open for 14% -> 18% of each run, Pallas kernels for 0% -> 14%
where the time goes in v1:
time: 624 us; the launch traced here: 616 us
  waiting for transfers between devices  240 us (38%)
  Pallas kernels  95.2 us (15%)
  local copies, waits for them, and re-layouts  92.3 us (15%)
  matrix products  86.7 us (14%)
  starting transfers between devices  47.3 us (8%)
  other arithmetic  37.6 us (6%)
  between operations  17.3 us (3%)
    ppermute x4, waiting for transfers between devices, to_clip(): lax.ppermute(pick(block[0], (parity + flip) % 2, 0), axes, routes[flip])  83.3 us
    all_gather x1, waiting for transfers between devices, body(): lax.all_gather(jnp.concatenate([w_query, w_key, w_value, vectors], 1), ax...  59.4 us
    ppermute x15, waiting for transfers between devices, scatter_sum(): lax.ppermute(pick(total, 1 - mine, 1).astype(bf16), 'grp', [(i, i ^ bit)...  59.3 us
    pallas_call x6, Pallas kernels, attend_back(): pl.pallas_call(attend_back_kernel, grid=(count, rows // Q_BLOCK), in_spec...  53.9 us
    pallas_call x1, Pallas kernels, attend(): pl.pallas_call(attend_kernel, grid=(pairs, rows // Q_BLOCK), in_specs=att...  41.3 us
    dot_general x1, matrix products, body(): hidden = jnp.dot(second_in, up_full, preferred_element_type=f32) + bu  28.6 us
    unnamed x185, local copies, waits for them, and re-layouts  20.6 us
    ppermute x4, waiting for transfers between devices, from_clip(): lax.ppermute(rows[flip * slice_len:(flip + 1) * slice_len], axes, back_ro...  20 us
  transfers between devices with their start and end apart: 54, of which 21 were waited for; matrix products, arithmetic and copies ran while one was open for 18% of the time, Pallas kernels for 14%

profile of v1, /device:TPU:9, one launch (start us, length us, event | category | flops | bytes accessed | tf_op | source)
XLA Modules:
  0.0 616.5 jit_solution(963566771071962533)
XLA Ops:
  18.4 59.4 %all-gather.3.cloned.1.call-done = bf16[768,2432]{1,0:T(8,128)(2,1)} async-done(((bf16[24,2432]{1,0:T(8,128)(2,1)}), bf16[768,2432]{1,0:T(8,128)(2,1)}) %all-gather.3.cloned.1.call-update) | async-done | bytes 3735568 | tf_op jit(solution)/shard_map/all_gather | solution.py:267
  77.9 2.4 constant_dynamic-slice_fusion.4
  80.6 3.3 collective-permute-start
  84.9 25.6 %collective-permute-done = bf16[384,768]{0,1:T(8,128)(2,1)S(1)} collective-permute-done((bf16[384,768]{0,1:T(8,128)(2,1)S(1)}, bf16[384,768]{0,1:T(8,128)(2,1)S(1)}, u32[]{:S(2)}, u32[]{:S(2)}) %collective-permute-start) | collective-permute-done | bytes 589856 | tf_op jit(solution)/shard_map/ppermute | solution.py:248
  110.5 12.5 %collective-permute-done.1 = bf16[384,768]{0,1:T(8,128)(2,1)S(1)} collective-permute-done((bf16[384,768]{0,1:T(8,128)(2,1)S(1)}, bf16[384,768]{0,1:T(8,128)(2,1)S(1)}, u32[]{:S(2)}, u32[]{:S(2)}) %collective-permute-start.1) | collective-permute-done | bytes 589856 | tf_op jit(solution)/shard_map/ppermute | solution.py:248
  126.5 4.3 add_convert_fusion.q_ref.ko_ref.vo_ref
  132.4 2.1 copy.182
  134.5 2.4 collective-permute-start.6
  137.0 2.1 copy.183
  139.1 2.5 collective-permute-start.7
  141.6 2.0 collective-permute-start.3
  147.1 18.1 %collective-permute-done.6 = bf16[384,768]{0,1:T(8,128)(2,1)} collective-permute-done((bf16[384,768]{0,1:T(8,128)(2,1)}, bf16[384,768]{0,1:T(8,128)(2,1)}, u32[]{:S(2)}, u32[]{:S(2)}) %collective-permute-start.6) | collective-permute-done | bytes 589856 | tf_op jit(solution)/shard_map/ppermute | solution.py:248
  165.1 1.9 constant_dynamic-update-slice_fusion.1
  167.1 27.2 %collective-permute-done.7 = bf16[384,768]{0,1:T(8,128)(2,1)} collective-permute-done((bf16[384,768]{0,1:T(8,128)(2,1)}, bf16[384,768]{0,1:T(8,128)(2,1)}, u32[]{:S(2)}, u32[]{:S(2)}) %collective-permute-start.7) | collective-permute-done | bytes 589856 | tf_op jit(solution)/shard_map/ppermute | solution.py:248
  194.2 1.9 constant_dynamic-update-slice_fusion
  197.1 1.8 add.440
  199.1 41.3 %shard_map.305 = (bf16[768,768]{1,0:T(8,128)(2,1)S(1)}, f32[6,8,768]{2,1,0:T(8,128)S(1)}) custom-call(bf16[768,2304]{1,0:T(8,128)(2,1)S(1)} %add_convert_fusion.q_ref.ko_ref.vo_ref, bf16[768,2304]{1,0:T(8,128)(2,1)S(1)} %add_convert_fusion.q_ref.ko_ref.vo_ref, bf16[768,1536]{1,0:T(8,128)(2,1)} %collective-permute-done.2.kx_ref.vx_ref, ...), custom_call_target="tpu_custom_call" | custom-call | flops 14495514624 | bytes 8257536 | tf_op jit(solution)/shard_map/pallas_call | solution.py:144
  242.9 3.2 fusion.112
  247.9 4.8 slice.153
  252.6 8.5 %reshape.221 = bf16[3072,768]{1,0:T(8,128)(2,1)} reshape(bf16[768,3072]{1,0:T(8,128)(2,1)} %slice.153) | data formatting | bytes 9437184 | tf_op jit(solution)/shard_map/reshape | solution.py:281
  261.2 28.6 %fusion.2 = (bf16[768,3072]{1,0:T(8,128)(2,1)}, f32[768,3072]{1,0:T(8,128)S(1)}) fusion(f32[3072]{0:T(1024)} %add.440, bf16[768,6912]{1,0:T(8,128)(2,1)} %all-gather.5.cloned.1.call-done, f32[768,768]{0,1:T(8,128)} %copy-done.46, f32[768]{0:T(1024)S(1)} %get-tuple-element.194, f32[768]{0:T(1024)S(1)} %get-tuple-element.195, f32[768]{0:T(1024)S(1)} %add_rsqrt_fusion, ...), kind=kOutput, calls=%fused_computation.4 | convolution fusion | flops 3782541312 | bytes 21258240 | tf_op jit(solution)/shard_map/dot_general | solution.py:302
  289.8 9.9 %convert_reduce_fusion = (f32[3072]{0:T(1024)}, bf16[768,3072]{1,0:T(8,128)(2,1)S(1)}) fusion(f32[768,3072]{1,0:T(8,128)S(1)} %get-tuple-element.249, f32[3072]{0:T(1024)S(1)} %copy-done.74, bf16[768,768]{0,1:T(8,128)(2,1)} %constant_dynamic-update-slice_fusion, bf16[3072,768]{1,0:T(8,128)(2,1)S(1)} %copy-done.56), kind=kOutput, calls=%fused_computation.11 | convolution fusion | flops 3654546432 | bytes 20078592 | tf_op jit(solution)/shard_map/dot_general | solution.py:310
  299.7 6.4 %fusion.106 = f32[768,3072]{1,0:T(8,128)} fusion(bf16[768,3072]{1,0:T(8,128)(2,1)S(1)} %get-tuple-element.255, f32[768,768]{0,1:T(8,128)S(1)} %copy-done.47, f32[768]{0:T(1024)S(1)} %get-tuple-element.194, f32[768]{0:T(1024)S(1)} %get-tuple-element.195, f32[768]{0:T(1024)S(1)} %add_rsqrt_fusion, f32[768]{0:T(1024)S(1)} %broadcast_multiply_fusion.4), kind=kOutput, calls=%fused_computation.245 | convolution fusion | flops 3626827776 | bytes 16527360 | tf_op jit(solution)/shard_map/dot_general | solution.py:312
  306.1 7.6 %fusion.114 = (f32[768]{0:T(1024)S(1)}, f32[768,768]{1,0:T(8,128)}) fusion(bf16[768,3072]{1,0:T(8,128)(2,1)S(1)} %get-tuple-element.255, bf16[768,6912]{1,0:T(8,128)(2,1)} %all-gather.5.cloned.1.call-done), kind=kOutput, calls=%fused_computation.253 | convolution fusion | flops 3624467712 | bytes 11799552 | tf_op jit(solution)/shard_map/dot_general | solution.py:314
  313.7 3.0 copy.184
  316.8 3.3 multiply_reduce_fusion
  320.6 2.7 convert_reduce_fusion.4
  324.7 3.3 convolution_convert_fusion.grad_ref
  328.0 9.3 %shard_map.306 = (bf16[768,128]{1,0:T(8,128)(2,1)S(1)}, bf16[768,128]{1,0:T(8,128)(2,1)S(1)}, bf16[768,128]{1,0:T(8,128)(2,1)S(1)}, bf16[768,128]{1,0:T(8,128)(2,1)}, bf16[768,128]{1,0:T(8,128)(2,1)S(1)}) custom-call(bf16[768,2304]{1,0:T(8,128)(2,1)S(1)} %add_convert_fusion.q_ref.ko_ref.vo_ref, bf16[768,2304]{1,0:T(8,128)(2,1)S(1)} %add_convert_fusion.q_ref.ko_ref.vo_ref, ...), custom_call_target="tpu_custom_call" | custom-call | flops 6039797760 | bytes 2359296 | tf_op jit(solution)/shard_map/pallas_call | solution.py:169
  338.8 8.9 %shard_map.307 = (bf16[768,128]{1,0:T(8,128)(2,1)S(1)}, bf16[768,128]{1,0:T(8,128)(2,1)S(1)}, bf16[768,128]{1,0:T(8,128)(2,1)S(1)}, bf16[768,128]{1,0:T(8,128)(2,1)}, bf16[768,128]{1,0:T(8,128)(2,1)S(1)}) custom-call(bf16[768,2304]{1,0:T(8,128)(2,1)S(1)} %add_convert_fusion.q_ref.ko_ref.vo_ref, bf16[768,2304]{1,0:T(8,128)(2,1)S(1)} %add_convert_fusion.q_ref.ko_ref.vo_ref, ...), custom_call_target="tpu_custom_call" | custom-call | flops 6039797760 | bytes 2359296 | tf_op jit(solution)/shard_map/pallas_call | solution.py:169
  350.3 8.9 %shard_map.308 = (bf16[768,128]{1,0:T(8,128)(2,1)S(1)}, bf16[768,128]{1,0:T(8,128)(2,1)S(1)}, bf16[768,128]{1,0:T(8,128)(2,1)S(1)}, bf16[768,128]{1,0:T(8,128)(2,1)}, bf16[768,128]{1,0:T(8,128)(2,1)S(1)}) custom-call(bf16[768,2304]{1,0:T(8,128)(2,1)S(1)} %add_convert_fusion.q_ref.ko_ref.vo_ref, bf16[768,2304]{1,0:T(8,128)(2,1)S(1)} %add_convert_fusion.q_ref.ko_ref.vo_ref, ...), custom_call_target="tpu_custom_call" | custom-call | flops 6039797760 | bytes 2359296 | tf_op jit(solution)/shard_map/pallas_call | solution.py:169
  360.5 8.9 %shard_map.309 = (bf16[768,128]{1,0:T(8,128)(2,1)S(1)}, bf16[768,128]{1,0:T(8,128)(2,1)S(1)}, bf16[768,128]{1,0:T(8,128)(2,1)S(1)}, bf16[768,128]{1,0:T(8,128)(2,1)}, bf16[768,128]{1,0:T(8,128)(2,1)S(1)}) custom-call(bf16[768,2304]{1,0:T(8,128)(2,1)S(1)} %add_convert_fusion.q_ref.ko_ref.vo_ref, bf16[768,2304]{1,0:T(8,128)(2,1)S(1)} %add_convert_fusion.q_ref.ko_ref.vo_ref, ...), custom_call_target="tpu_custom_call" | custom-call | flops 6039797760 | bytes 2359296 | tf_op jit(solution)/shard_map/pallas_call | solution.py:169
  371.2 9.5 %shard_map.310 = (bf16[768,128]{1,0:T(8,128)(2,1)S(1)}, bf16[768,128]{1,0:T(8,128)(2,1)S(1)}, bf16[768,128]{1,0:T(8,128)(2,1)S(1)}, bf16[768,128]{1,0:T(8,128)(2,1)}, bf16[768,128]{1,0:T(8,128)(2,1)S(1)}) custom-call(bf16[768,2304]{1,0:T(8,128)(2,1)S(1)} %add_convert_fusion.q_ref.ko_ref.vo_ref, bf16[768,2304]{1,0:T(8,128)(2,1)S(1)} %add_convert_fusion.q_ref.ko_ref.vo_ref, ...), custom_call_target="tpu_custom_call" | custom-call | flops 6039797760 | bytes 2359296 | tf_op jit(solution)/shard_map/pallas_call | solution.py:169
  380.9 7.9 %fusion.115 = f32[3072,768]{1,0:T(8,128)} fusion(bf16[768,3072]{1,0:T(8,128)(2,1)S(1)} %bitcast.226, bf16[768,768]{0,1:T(8,128)(2,1)} %constant_dynamic-update-slice_fusion), kind=kOutput, calls=%fused_computation.254 | convolution fusion | flops 3623878656 | bytes 15335424 | tf_op jit(solution)/shard_map/dot_general | solution.py:308
  388.8 4.2 fusion.39
  393.9 4.3 add_convert_fusion.1
  402.2 8.4 %shard_map.311 = (bf16[768,128]{1,0:T(8,128)(2,1)S(1)}, bf16[768,128]{1,0:T(8,128)(2,1)S(1)}, bf16[768,128]{1,0:T(8,128)(2,1)S(1)}, bf16[768,128]{1,0:T(8,128)(2,1)S(1)}, bf16[768,128]{1,0:T(8,128)(2,1)S(1)}) custom-call(bf16[768,2304]{1,0:T(8,128)(2,1)S(1)} %add_convert_fusion.q_ref.ko_ref.vo_ref, ...), custom_call_target="tpu_custom_call" | custom-call | flops 6039797760 | bytes 2359296 | tf_op jit(solution)/shard_map/pallas_call | solution.py:169
  416.4 4.1 fusion.40
  428.7 1.9 collective-permute-start.4
  431.2 5.0 fusion.113
  437.4 2.1 copy.185
  444.6 3.2 concatenate.31
  448.9 4.3 collective-permute-start.46
  453.2 5.2 fusion.103
  460.5 2.8 collective-permute-done.47
  466.2 3.8 collective-permute-start.50
  471.1 2.5 collective-permute-start.40
  474.1 2.0 collective-permute-start.22
  477.6 3.6 collective-permute-start.20
  487.2 7.9 %collective-permute-done.20 = bf16[384,768]{0,1:T(8,128)(2,1)S(1)} collective-permute-done((bf16[384,768]{0,1:T(8,128)(2,1)}, bf16[384,768]{0,1:T(8,128)(2,1)S(1)}, u32[]{:S(2)}, u32[]{:S(2)}) %collective-permute-start.20) | collective-permute-done | bytes 589856 | tf_op jit(solution)/shard_map/ppermute | solution.py:256
  495.7 12.1 %collective-permute-done.21 = bf16[384,768]{0,1:T(8,128)(2,1)S(1)} collective-permute-done((bf16[384,768]{0,1:T(8,128)(2,1)}, bf16[384,768]{0,1:T(8,128)(2,1)S(1)}, u32[]{:S(2)}, u32[]{:S(2)}) %collective-permute-start.21) | collective-permute-done | bytes 589856 | tf_op jit(solution)/shard_map/ppermute | solution.py:256
  511.4 2.9 bitcast_add_fusion.2
  516.5 3.7 bitcast_add_fusion
  520.3 6.0 collective-permute-done.23
  527.9 2.6 bitcast_add_fusion.1
  530.7 6.6 %collective-permute-done.24 = bf16[1,96,2304]{2,1,0:T(8,128)(2,1)S(1)} collective-permute-done((bf16[1,96,2304]{2,1,0:T(8,128)(2,1)S(1)}, bf16[1,96,2304]{2,1,0:T(8,128)(2,1)S(1)}, u32[]{:S(2)}, u32[]{:S(2)}) %collective-permute-start.24) | collective-permute-done | bytes 442400 | tf_op jit(solution)/shard_map/ppermute | solution.py:199
  537.3 2.3 collective-permute-start.35
  542.0 1.7 collective-permute-done.25
  544.5 2.6 collective-permute-done.27
  547.1 6.8 %collective-permute-done.41 = bf16[2,384,768]{2,1,0:T(8,128)(2,1)S(1)} collective-permute-done((bf16[2,384,768]{2,1,0:T(8,128)(2,1)S(1)}, bf16[2,384,768]{2,1,0:T(8,128)(2,1)S(1)}, u32[]{:S(2)}, u32[]{:S(2)}) %collective-permute-start.41) | collective-permute-done | bytes 1179680 | tf_op jit(solution)/shard_map/ppermute | solution.py:199
  554.9 24.3 %collective-permute-done.35 = bf16[2,96,3072]{2,1,0:T(8,128)(2,1)S(1)} collective-permute-done((bf16[2,96,3072]{2,1,0:T(8,128)(2,1)S(1)}, bf16[2,96,3072]{2,1,0:T(8,128)(2,1)S(1)}, u32[]{:S(2)}, u32[]{:S(2)}) %collective-permute-start.35) | collective-permute-done | bytes 1179680 | tf_op jit(solution)/shard_map/ppermute | solution.py:199
  582.7 11.2 %collective-permute-done.36 = bf16[1,96,3072]{2,1,0:T(8,128)(2,1)S(1)} collective-permute-done((bf16[1,96,3072]{2,1,0:T(8,128)(2,1)S(1)}, bf16[1,96,3072]{2,1,0:T(8,128)(2,1)S(1)}, u32[]{:S(2)}, u32[]{:S(2)}) %collective-permute-start.36) | collective-permute-done | bytes 589856 | tf_op jit(solution)/shard_map/ppermute | solution.py:199
  595.6 5.5 collective-permute-done.45
  601.9 6.5 %collective-permute-done.39 = bf16[24,3072]{1,0:T(8,128)(2,1)S(1)} collective-permute-done((bf16[24,3072]{1,0:T(8,128)(2,1)S(1)}, bf16[24,3072]{1,0:T(8,128)(2,1)S(1)}, u32[]{:S(2)}, u32[]{:S(2)}) %collective-permute-start.39) | collective-permute-done | bytes 147488 | tf_op jit(solution)/shard_map/ppermute | solution.py:207
  (377 shorter events, 93.5 us)
Async XLA Ops:
  7.2 70.7 %copy-start.62 = (bf16[1,2,384,768]{3,2,1,0:T(8,128)(2,1)S(1)}, bf16[1,2,384,768]{3,2,1,0:T(8,128)(2,1)}, u32[]{:S(2)}) copy-start(bf16[1,2,384,768]{3,2,1,0:T(8,128)(2,1)} %param.20) | copy-start | bytes 3538948
  7.2 70.6 %all-gather.3.cloned.1.call-start = ((), (), s32[]{:S(2)}) async-start(), calls=%async_computation | async-start | bytes 3852288 | tf_op jit(solution)/shard_map/all_gather | solution.py:267
  15.7 227.3 %all-gather.5.cloned.1.call-start = ((), (), s32[]{:S(2)}) async-start(), calls=%async_computation.1 | async-start | bytes 10948608 | tf_op jit(solution)/shard_map/all_gather | solution.py:272
  80.6 29.9 %collective-permute-start = (bf16[384,768]{0,1:T(8,128)(2,1)S(1)}, bf16[384,768]{0,1:T(8,128)(2,1)S(1)}, u32[]{:S(2)}, u32[]{:S(2)}) collective-permute-start(bf16[384,768]{0,1:T(8,128)(2,1)S(1)} %bitcast.213), channel_id=1, source_target_pairs={{0,0},{1,1},{2,4},{3,5},{4,2},{5,3},{6,6},{7,7},{8,8},{9,9},{10,12... | collective-permute-start | bytes 1769480 | tf_op jit(solution)/shard_map/ppermute | solution.py:248
  84.2 38.8 %collective-permute-start.1 = (bf16[384,768]{0,1:T(8,128)(2,1)S(1)}, bf16[384,768]{0,1:T(8,128)(2,1)S(1)}, u32[]{:S(2)}, u32[]{:S(2)}) collective-permute-start(bf16[384,768]{0,1:T(8,128)(2,1)S(1)} %bitcast.214), channel_id=1, source_target_pairs={{0,1},{1,0},{2,5},{3,4},{4,3},{5,2},{6,7},{7,6},{8,9},{9,8},{10,13... | collective-permute-start | bytes 1769480 | tf_op jit(solution)/shard_map/ppermute | solution.py:248
  110.5 16.0 %copy-start.50 = (bf16[384,768]{0,1:T(8,128)(2,1)}, bf16[384,768]{0,1:T(8,128)(2,1)S(1)}, u32[]{:S(2)}) copy-start(bf16[384,768]{0,1:T(8,128)(2,1)S(1)} %collective-permute-done) | copy-start | bytes 1769476
  132.4 66.5 %collective-permute-start.2 = (bf16[768,1536]{1,0:T(8,128)(2,1)}, bf16[768,1536]{1,0:T(8,128)(2,1)}, u32[]{:S(2)}, u32[]{:S(2)}) collective-permute-start(bf16[768,1536]{1,0:T(8,128)(2,1)} %slice.146), channel_id=1, source_target_pairs={{0,4},{4,0},{8,12},{12,8},{16,20},{20,16},{24,28},{28,24},{1,5},{5... | collective-permute-start | bytes 7077896 | tf_op jit(solution)/shard_map/ppermute | solution.py:297
  134.5 30.6 %collective-permute-start.6 = (bf16[384,768]{0,1:T(8,128)(2,1)}, bf16[384,768]{0,1:T(8,128)(2,1)}, u32[]{:S(2)}, u32[]{:S(2)}) collective-permute-start(bf16[384,768]{0,1:T(8,128)(2,1)} %bitcast.211), channel_id=1, source_target_pairs={{0,0},{1,1},{2,4},{3,5},{4,2},{5,3},{6,6},{7,7},{8,8},{9,9},{10,12... | collective-permute-start | bytes 1769480 | tf_op jit(solution)/shard_map/ppermute | solution.py:248
  139.1 55.1 %collective-permute-start.7 = (bf16[384,768]{0,1:T(8,128)(2,1)}, bf16[384,768]{0,1:T(8,128)(2,1)}, u32[]{:S(2)}, u32[]{:S(2)}) collective-permute-start(bf16[384,768]{0,1:T(8,128)(2,1)} %bitcast.212), channel_id=1, source_target_pairs={{0,1},{1,0},{2,5},{3,4},{4,3},{5,2},{6,7},{7,6},{8,9},{9,8},{10,13... | collective-permute-start | bytes 1769480 | tf_op jit(solution)/shard_map/ppermute | solution.py:248
  141.6 2.9 collective-permute-start.3
  147.0 49.1 %copy-start.45 = (f32[128,768]{0,1:T(8,128)S(1)}, f32[128,768]{0,1:T(8,128)}, u32[]{:S(2)}) copy-start(f32[128,768]{0,1:T(8,128)} %copy-done.44) | copy-start | bytes 1179652
  261.2 28.6 %copy-start.56 = (bf16[3072,768]{1,0:T(8,128)(2,1)S(1)}, bf16[3072,768]{1,0:T(8,128)(2,1)}, u32[]{:S(2)}) copy-start(bf16[3072,768]{1,0:T(8,128)(2,1)} %reshape.221) | copy-start | bytes 14155780
  261.2 28.6 %copy-start.74 = (f32[3072]{0:T(1024)S(1)}, f32[3072]{0:T(1024)}, u32[]{:S(2)}) copy-start(f32[3072]{0:T(1024)} %add.440) | copy-start | bytes 36868
  324.7 68.3 %copy-start.60 = (f32[768,768]{1,0:T(8,128)}, f32[768,768]{1,0:T(8,128)S(1)}, u32[]{:S(2)}) copy-start(f32[768,768]{1,0:T(8,128)S(1)} %fusion.100) | copy-start | bytes 7077892
  338.8 81.7 %collective-permute-start.8 = (bf16[768,128]{1,0:T(8,128)(2,1)}, bf16[768,128]{1,0:T(8,128)(2,1)}, u32[]{:S(2)}, u32[]{:S(2)}) collective-permute-start(bf16[768,128]{1,0:T(8,128)(2,1)} %get-tuple-element.62), channel_id=1, source_target_pairs={{0,4},{4,0},{8,12},{12,8},{16,20},{20,16},{24,28},{28,24},{1,5},{5... | collective-permute-start | bytes 589832 | tf_op jit(solution)/shard_map/ppermute | solution.py:337
  349.7 72.4 %collective-permute-start.9 = (bf16[768,128]{1,0:T(8,128)(2,1)}, bf16[768,128]{1,0:T(8,128)(2,1)}, u32[]{:S(2)}, u32[]{:S(2)}) collective-permute-start(bf16[768,128]{1,0:T(8,128)(2,1)} %get-tuple-element.64), channel_id=1, source_target_pairs={{0,4},{4,0},{8,12},{12,8},{16,20},{20,16},{24,28},{28,24},{1,5},{5... | collective-permute-start | bytes 589832 | tf_op jit(solution)/shard_map/ppermute | solution.py:337
  360.5 63.0 %collective-permute-start.10 = (bf16[768,128]{1,0:T(8,128)(2,1)}, bf16[768,128]{1,0:T(8,128)(2,1)}, u32[]{:S(2)}, u32[]{:S(2)}) collective-permute-start(bf16[768,128]{1,0:T(8,128)(2,1)} %get-tuple-element.66), channel_id=1, source_target_pairs={{0,4},{4,0},{8,12},{12,8},{16,20},{20,16},{24,28},{28,24},{1,5},{5... | collective-permute-start | bytes 589832 | tf_op jit(solution)/shard_map/ppermute | solution.py:337
  370.7 54.2 %collective-permute-start.11 = (bf16[768,128]{1,0:T(8,128)(2,1)}, bf16[768,128]{1,0:T(8,128)(2,1)}, u32[]{:S(2)}, u32[]{:S(2)}) collective-permute-start(bf16[768,128]{1,0:T(8,128)(2,1)} %get-tuple-element.68), channel_id=1, source_target_pairs={{0,4},{4,0},{8,12},{12,8},{16,20},{20,16},{24,28},{28,24},{1,5},{5... | collective-permute-start | bytes 589832 | tf_op jit(solution)/shard_map/ppermute | solution.py:337
  371.2 22.6 %slice-start.3 = ((s8[4718592]{0:T(1024)(128)(4,1)}), s8[524288]{0:T(1024)(128)(4,1)S(1)}, s32[]{:S(2)}) async-start(s8[4718592]{0:T(1024)(128)(4,1)} %bitcast.190), calls=%async_computation.5 | async-start | bytes 1048576
  380.7 45.5 %collective-permute-start.12 = (bf16[768,128]{1,0:T(8,128)(2,1)}, bf16[768,128]{1,0:T(8,128)(2,1)}, u32[]{:S(2)}, u32[]{:S(2)}) collective-permute-start(bf16[768,128]{1,0:T(8,128)(2,1)} %get-tuple-element.70), channel_id=1, source_target_pairs={{0,4},{4,0},{8,12},{12,8},{16,20},{20,16},{24,28},{28,24},{1,5},{5... | collective-permute-start | bytes 589832 | tf_op jit(solution)/shard_map/ppermute | solution.py:337
  380.8 13.0 %slice-start.4 = ((s8[4718592]{0:T(1024)(128)(4,1)}), s8[4194304]{0:T(1024)(128)(4,1)S(1)}, s32[]{:S(2)}) async-start(s8[4718592]{0:T(1024)(128)(4,1)} %bitcast.190), calls=%async_computation.6 | async-start | bytes 8388608
  402.2 13.0 %copy-start.73 = (f32[3072]{0:T(1024)S(1)}, f32[3072]{0:T(1024)}, u32[]{:S(2)}) copy-start(f32[3072]{0:T(1024)} %get-tuple-element.254) | copy-start | bytes 36868
  420.6 7.3 %collective-permute-start.13 = (bf16[768,128]{1,0:T(8,128)(2,1)S(1)}, bf16[768,128]{1,0:T(8,128)(2,1)S(1)}, u32[]{:S(2)}, u32[]{:S(2)}) collective-permute-start(bf16[768,128]{1,0:T(8,128)(2,1)S(1)} %copy-done.39), channel_id=1, source_target_pairs={{0,4},{4,0},{8,12},{12,8},{16,20},{20,16},{24,28},{28,24},{1,5},{5... | collective-permute-start | bytes 589832 | tf_op jit(solution)/shard_map/ppermute | solution.py:337
  422.2 6.0 collective-permute-start.14
  423.5 5.2 collective-permute-start.15
  425.0 5.8 collective-permute-start.16
  426.3 4.6 collective-permute-start.17
  427.9 3.1 collective-permute-start.18
  428.2 2.9 collective-permute-start.19
  428.7 48.9 %collective-permute-start.4 = (bf16[384,768]{0,1:T(8,128)(2,1)}, bf16[384,768]{0,1:T(8,128)(2,1)}, u32[]{:S(2)}, u32[]{:S(2)}) collective-permute-start(bf16[384,768]{0,1:T(8,128)(2,1)} %get-tuple-element.226), channel_id=1, source_target_pairs={{0,0},{1,1},{4,2},{5,3},{2,4},{3,5},{6,6},{7,7},{8,8},{9,9},{12,10... | collective-permute-start | bytes 1769480 | tf_op jit(solution)/shard_map/ppermute | solution.py:256
  430.7 50.5 %collective-permute-start.5 = (bf16[384,768]{0,1:T(8,128)(2,1)}, bf16[384,768]{0,1:T(8,128)(2,1)}, u32[]{:S(2)}, u32[]{:S(2)}) collective-permute-start(bf16[384,768]{0,1:T(8,128)(2,1)} %get-tuple-element.227), channel_id=1, source_target_pairs={{1,0},{0,1},{5,2},{4,3},{3,4},{2,5},{7,6},{6,7},{9,8},{8,9},{13,10... | collective-permute-start | bytes 1769480 | tf_op jit(solution)/shard_map/ppermute | solution.py:256
  448.9 10.9 %collective-permute-start.46 = (bf16[4,96,128]{2,1,0:T(8,128)(2,1)S(1)}, bf16[4,96,128]{2,1,0:T(8,128)(2,1)S(1)}, u32[]{:S(2)}, u32[]{:S(2)}) collective-permute-start(bf16[4,96,128]{2,1,0:T(8,128)(2,1)S(1)} %fusion.78), channel_id=1, source_target_pairs={{0,4},{4,0},{8,12},{12,8},{16,20},{20,16},{24,28},{28,24},{1,5},{5... | collective-permute-start | bytes 294920 | tf_op jit(solution)/shard_map/ppermute | solution.py:199
  459.9 3.4 collective-permute-start.47
  463.3 2.7 collective-permute-start.48
  466.1 5.0 collective-permute-start.49
  466.2 7.5 %collective-permute-start.50 = (bf16[24,128]{1,0:T(8,128)(2,1)S(1)}, bf16[24,128]{1,0:T(8,128)(2,1)S(1)}, u32[]{:S(2)}, u32[]{:S(2)}) collective-permute-start(bf16[24,128]{1,0:T(8,128)(2,1)S(1)} %get-tuple-element.241), channel_id=1, source_target_pairs={{0,2},{1,3},{2,0},{3,1},{4,6},{5,7},{6,4},{7,5},{8,10},{9,11},{10,... | collective-permute-start | bytes 18440 | tf_op jit(solution)/shard_map/ppermute | solution.py:207
  470.0 4.2 collective-permute-start.51
  471.1 43.9 %collective-permute-start.40 = (bf16[4,384,768]{2,1,0:T(8,128)(2,1)}, bf16[4,384,768]{2,1,0:T(8,128)(2,1)}, u32[]{:S(2)}, u32[]{:S(2)}) collective-permute-start(bf16[4,384,768]{2,1,0:T(8,128)(2,1)} %fusion.40), channel_id=1, source_target_pairs={{0,4},{4,0},{8,12},{12,8},{16,20},{20,16},{24,28},{28,24},{1,5},{5... | collective-permute-start | bytes 7077896 | tf_op jit(solution)/shard_map/ppermute | solution.py:199
  473.7 9.3 %collective-permute-start.28 = (bf16[4,96,768]{2,1,0:T(8,128)(2,1)S(1)}, bf16[4,96,768]{2,1,0:T(8,128)(2,1)S(1)}, u32[]{:S(2)}, u32[]{:S(2)}) collective-permute-start(bf16[4,96,768]{2,1,0:T(8,128)(2,1)S(1)} %copy-done.63), channel_id=1, source_target_pairs={{0,4},{4,0},{8,12},{12,8},{16,20},{20,16},{24,28},{28,24},{1,5},{5... | collective-permute-start | bytes 1769480 | tf_op jit(solution)/shard_map/ppermute | solution.py:199
  474.1 37.2 %collective-permute-start.22 = (bf16[4,96,2304]{2,1,0:T(8,128)(2,1)}, bf16[4,96,2304]{2,1,0:T(8,128)(2,1)}, u32[]{:S(2)}, u32[]{:S(2)}) collective-permute-start(bf16[4,96,2304]{2,1,0:T(8,128)(2,1)} %fusion.41), channel_id=1, source_target_pairs={{0,4},{4,0},{8,12},{12,8},{16,20},{20,16},{24,28},{28,24},{1,5},{5... | collective-permute-start | bytes 5308424 | tf_op jit(solution)/shard_map/ppermute | solution.py:199
  477.6 17.5 %collective-permute-start.20 = (bf16[384,768]{0,1:T(8,128)(2,1)}, bf16[384,768]{0,1:T(8,128)(2,1)S(1)}, u32[]{:S(2)}, u32[]{:S(2)}) collective-permute-start(bf16[384,768]{0,1:T(8,128)(2,1)} %get-tuple-element.220), channel_id=1, source_target_pairs={{0,0},{1,1},{4,2},{5,3},{2,4},{3,5},{6,6},{7,7},{8,8},{9,9},{12,10... | collective-permute-start | bytes 1769480 | tf_op jit(solution)/shard_map/ppermute | solution.py:256
  481.2 26.6 %collective-permute-start.21 = (bf16[384,768]{0,1:T(8,128)(2,1)}, bf16[384,768]{0,1:T(8,128)(2,1)S(1)}, u32[]{:S(2)}, u32[]{:S(2)}) collective-permute-start(bf16[384,768]{0,1:T(8,128)(2,1)} %get-tuple-element.221), channel_id=1, source_target_pairs={{1,0},{0,1},{5,2},{4,3},{3,4},{2,5},{7,6},{6,7},{9,8},{8,9},{13,10... | collective-permute-start | bytes 1769480 | tf_op jit(solution)/shard_map/ppermute | solution.py:256
  483.8 42.8 %collective-permute-start.34 = (bf16[4,96,3072]{2,1,0:T(8,128)(2,1)}, bf16[4,96,3072]{2,1,0:T(8,128)(2,1)}, u32[]{:S(2)}, u32[]{:S(2)}) collective-permute-start(bf16[4,96,3072]{2,1,0:T(8,128)(2,1)} %fusion.39), channel_id=1, source_target_pairs={{0,4},{4,0},{8,12},{12,8},{16,20},{20,16},{24,28},{28,24},{1,5},{5... | collective-permute-start | bytes 7077896 | tf_op jit(solution)/shard_map/ppermute | solution.py:199
  495.1 14.4 %collective-permute-start.29 = (bf16[2,96,768]{2,1,0:T(8,128)(2,1)}, bf16[2,96,768]{2,1,0:T(8,128)(2,1)}, u32[]{:S(2)}, u32[]{:S(2)}) collective-permute-start(bf16[2,96,768]{2,1,0:T(8,128)(2,1)} %fusion.48), channel_id=1, source_target_pairs={{0,8},{4,12},{8,0},{12,4},{16,24},{20,28},{24,16},{28,20},{1,9},{5... | collective-permute-start | bytes 884744 | tf_op jit(solution)/shard_map/ppermute | solution.py:199
  510.5 4.4 collective-permute-start.30
  514.4 12.0 %collective-permute-start.23 = (bf16[2,96,2304]{2,1,0:T(8,128)(2,1)S(1)}, bf16[2,96,2304]{2,1,0:T(8,128)(2,1)S(1)}, u32[]{:S(2)}, u32[]{:S(2)}) collective-permute-start(bf16[2,96,2304]{2,1,0:T(8,128)(2,1)S(1)} %fusion.46), channel_id=1, source_target_pairs={{0,8},{4,12},{8,0},{12,4},{16,24},{20,28},{24,16},{28,20},{1,9},{5... | collective-permute-start | bytes 2654216 | tf_op jit(solution)/shard_map/ppermute | solution.py:199
  514.9 24.8 %collective-permute-start.31 = (bf16[24,768]{1,0:T(8,128)(2,1)S(1)}, bf16[24,768]{1,0:T(8,128)(2,1)S(1)}, u32[]{:S(2)}, u32[]{:S(2)}) collective-permute-start(bf16[24,768]{1,0:T(8,128)(2,1)S(1)} %get-tuple-element.233), channel_id=1, source_target_pairs={{0,1},{1,2},{2,3},{3,0},{4,5},{5,6},{6,7},{7,4},{8,9},{9,10},{10,1... | collective-permute-start | bytes 110600 | tf_op jit(solution)/shard_map/ppermute | solution.py:207
  515.0 24.8 %collective-permute-start.32 = (bf16[24,768]{1,0:T(8,128)(2,1)S(1)}, bf16[24,768]{1,0:T(8,128)(2,1)S(1)}, u32[]{:S(2)}, u32[]{:S(2)}) collective-permute-start(bf16[24,768]{1,0:T(8,128)(2,1)S(1)} %get-tuple-element.235), channel_id=1, source_target_pairs={{0,2},{1,3},{2,0},{3,1},{4,6},{5,7},{6,4},{7,5},{8,10},{9,11},{10,... | collective-permute-start | bytes 110600 | tf_op jit(solution)/shard_map/ppermute | solution.py:207
  515.1 24.8 %collective-permute-start.33 = (bf16[24,768]{1,0:T(8,128)(2,1)S(1)}, bf16[24,768]{1,0:T(8,128)(2,1)S(1)}, u32[]{:S(2)}, u32[]{:S(2)}) collective-permute-start(bf16[24,768]{1,0:T(8,128)(2,1)S(1)} %get-tuple-element.234), channel_id=1, source_target_pairs={{0,3},{1,0},{2,1},{3,2},{4,7},{5,4},{6,5},{7,6},{8,11},{9,8},{10,9... | collective-permute-start | bytes 110600 | tf_op jit(solution)/shard_map/ppermute | solution.py:207
  516.5 11.4 %slice-start.1 = ((s8[9437184]{0:T(1024)(128)(4,1)}), s8[4194304]{0:T(1024)(128)(4,1)S(1)}, s32[]{:S(2)}) async-start(s8[9437184]{0:T(1024)(128)(4,1)} %bitcast.185), calls=%async_computation.3 | async-start | bytes 8388608
  526.3 27.6 %collective-permute-start.41 = (bf16[2,384,768]{2,1,0:T(8,128)(2,1)S(1)}, bf16[2,384,768]{2,1,0:T(8,128)(2,1)S(1)}, u32[]{:S(2)}, u32[]{:S(2)}) collective-permute-start(bf16[2,384,768]{2,1,0:T(8,128)(2,1)S(1)} %fusion.43), channel_id=1, source_target_pairs={{0,8},{4,12},{8,0},{12,4},{16,24},{20,28},{24,16},{28,20},{1,9},{5... | collective-permute-start | bytes 3538952 | tf_op jit(solution)/shard_map/ppermute | solution.py:199
  526.6 10.8 %collective-permute-start.24 = (bf16[1,96,2304]{2,1,0:T(8,128)(2,1)S(1)}, bf16[1,96,2304]{2,1,0:T(8,128)(2,1)S(1)}, u32[]{:S(2)}, u32[]{:S(2)}) collective-permute-start(bf16[1,96,2304]{2,1,0:T(8,128)(2,1)S(1)} %dynamic-slice_convert_fusion.6), channel_id=1, source_target_pairs={{0,16},{4,20},{8,24},{12,28},{16,0},{20,4},{24,8},{28,12},{1,17},{... | collective-permute-start | bytes 1327112 | tf_op jit(solution)/shard_map/ppermute | solution.py:199
  537.3 41.9 %collective-permute-start.35 = (bf16[2,96,3072]{2,1,0:T(8,128)(2,1)S(1)}, bf16[2,96,3072]{2,1,0:T(8,128)(2,1)S(1)}, u32[]{:S(2)}, u32[]{:S(2)}) collective-permute-start(bf16[2,96,3072]{2,1,0:T(8,128)(2,1)S(1)} %fusion.42), channel_id=1, source_target_pairs={{0,8},{4,12},{8,0},{12,4},{16,24},{20,28},{24,16},{28,20},{1,9},{5... | collective-permute-start | bytes 3538952 | tf_op jit(solution)/shard_map/ppermute | solution.py:199
  539.8 3.9 collective-permute-start.25
  539.8 4.7 collective-permute-start.26
  539.9 7.1 %collective-permute-start.27 = (bf16[24,2304]{1,0:T(8,128)(2,1)S(1)}, bf16[24,2304]{1,0:T(8,128)(2,1)S(1)}, u32[]{:S(2)}, u32[]{:S(2)}) collective-permute-start(bf16[24,2304]{1,0:T(8,128)(2,1)S(1)} %get-tuple-element.231), channel_id=1, source_target_pairs={{0,3},{1,0},{2,1},{3,2},{4,7},{5,4},{6,5},{7,6},{8,11},{9,8},{10,9... | collective-permute-start | bytes 331784 | tf_op jit(solution)/shard_map/ppermute | solution.py:207
  554.3 26.7 %collective-permute-start.42 = (bf16[1,384,768]{2,1,0:T(8,128)(2,1)S(1)}, bf16[1,384,768]{2,1,0:T(8,128)(2,1)S(1)}, u32[]{:S(2)}, u32[]{:S(2)}) collective-permute-start(bf16[1,384,768]{2,1,0:T(8,128)(2,1)S(1)} %dynamic-slice_convert_fusion.3), channel_id=1, source_target_pairs={{0,16},{4,20},{8,24},{12,28},{16,0},{20,4},{24,8},{28,12},{1,17},{... | collective-permute-start | bytes 1769480 | tf_op jit(solution)/shard_map/ppermute | solution.py:199
  579.7 14.2 %collective-permute-start.36 = (bf16[1,96,3072]{2,1,0:T(8,128)(2,1)S(1)}, bf16[1,96,3072]{2,1,0:T(8,128)(2,1)S(1)}, u32[]{:S(2)}, u32[]{:S(2)}) collective-permute-start(bf16[1,96,3072]{2,1,0:T(8,128)(2,1)S(1)} %dynamic-slice_convert_fusion.4), channel_id=1, source_target_pairs={{0,16},{4,20},{8,24},{12,28},{16,0},{20,4},{24,8},{28,12},{1,17},{... | collective-permute-start | bytes 1769480 | tf_op jit(solution)/shard_map/ppermute | solution.py:199
  581.2 13.0 %collective-permute-start.43 = (bf16[96,768]{1,0:T(8,128)(2,1)S(1)}, bf16[96,768]{1,0:T(8,128)(2,1)S(1)}, u32[]{:S(2)}, u32[]{:S(2)}) collective-permute-start(bf16[96,768]{1,0:T(8,128)(2,1)S(1)} %get-tuple-element.212), channel_id=1, source_target_pairs={{0,1},{1,2},{2,3},{3,0},{4,5},{5,6},{6,7},{7,4},{8,9},{9,10},{10,1... | collective-permute-start | bytes 442376 | tf_op jit(solution)/shard_map/ppermute | solution.py:207
  581.3 14.3 %collective-permute-start.44 = (bf16[96,768]{1,0:T(8,128)(2,1)S(1)}, bf16[96,768]{1,0:T(8,128)(2,1)S(1)}, u32[]{:S(2)}, u32[]{:S(2)}) collective-permute-start(bf16[96,768]{1,0:T(8,128)(2,1)S(1)} %get-tuple-element.214), channel_id=1, source_target_pairs={{0,2},{1,3},{2,0},{3,1},{4,6},{5,7},{6,4},{7,5},{8,10},{9,11},{10,... | collective-permute-start | bytes 442376 | tf_op jit(solution)/shard_map/ppermute | solution.py:207
  581.3 19.8 %collective-permute-start.45 = (bf16[96,768]{1,0:T(8,128)(2,1)S(1)}, bf16[96,768]{1,0:T(8,128)(2,1)S(1)}, u32[]{:S(2)}, u32[]{:S(2)}) collective-permute-start(bf16[96,768]{1,0:T(8,128)(2,1)S(1)} %get-tuple-element.213), channel_id=1, source_target_pairs={{0,3},{1,0},{2,1},{3,2},{4,7},{5,4},{6,5},{7,6},{8,11},{9,8},{10,9... | collective-permute-start | bytes 442376 | tf_op jit(solution)/shard_map/ppermute | solution.py:207
  594.1 7.8 %collective-permute-start.37 = (bf16[24,3072]{1,0:T(8,128)(2,1)S(1)}, bf16[24,3072]{1,0:T(8,128)(2,1)S(1)}, u32[]{:S(2)}, u32[]{:S(2)}) collective-permute-start(bf16[24,3072]{1,0:T(8,128)(2,1)S(1)} %get-tuple-element.215), channel_id=1, source_target_pairs={{0,1},{1,2},{2,3},{3,0},{4,5},{5,6},{6,7},{7,4},{8,9},{9,10},{10,1... | collective-permute-start | bytes 442376 | tf_op jit(solution)/shard_map/ppermute | solution.py:207
  594.1 7.8 %collective-permute-start.38 = (bf16[24,3072]{1,0:T(8,128)(2,1)S(1)}, bf16[24,3072]{1,0:T(8,128)(2,1)S(1)}, u32[]{:S(2)}, u32[]{:S(2)}) collective-permute-start(bf16[24,3072]{1,0:T(8,128)(2,1)S(1)} %get-tuple-element.217), channel_id=1, source_target_pairs={{0,2},{1,3},{2,0},{3,1},{4,6},{5,7},{6,4},{7,5},{8,10},{9,11},{10,... | collective-permute-start | bytes 442376 | tf_op jit(solution)/shard_map/ppermute | solution.py:207
  594.2 14.2 %collective-permute-start.39 = (bf16[24,3072]{1,0:T(8,128)(2,1)S(1)}, bf16[24,3072]{1,0:T(8,128)(2,1)S(1)}, u32[]{:S(2)}, u32[]{:S(2)}) collective-permute-start(bf16[24,3072]{1,0:T(8,128)(2,1)S(1)} %get-tuple-element.216), channel_id=1, source_target_pairs={{0,3},{1,0},{2,1},{3,2},{4,7},{5,4},{6,5},{7,6},{8,11},{9,8},{10,9... | collective-permute-start | bytes 442376 | tf_op jit(solution)/shard_map/ppermute | solution.py:207
  (78 other events, 369.7 us)
Sparse Core Ops, SparseCore 0:
  15.8 61.9 all-gather.2
  80.6 109.4 all-gather.4

commit v2 on v1

--- a/solution.py
+++ b/solution.py
@@ -289,13 +289,19 @@
     )
 
     token_rows = to_clip(inputs).astype(f32)
-    grad_top = to_clip(cotangent)
     normed_one, inverse_one = standardize(token_rows)
     first_in = (normed_one * gain_first + shift_first).astype(bf16)
     b_qkv = jnp.concatenate([bq, jnp.zeros_like(bq), bv])
     qkv = (jnp.dot(first_in, w_qkv, preferred_element_type=f32) + b_qkv).astype(bf16)
     kv_other = lax.ppermute(qkv[:, width:], "grp", swap)
+    kv_other, cotangent = lax.optimization_barrier((kv_other, cotangent))
+    parts = [
+        lax.ppermute(pick(cotangent[0], (parity + flip) % 2, 0), axes, routes[flip])
+        for flip in range(2)
+    ]
     mixed_low, lse = attend(qkv, kv_other, bias)
+    mixed_low, *parts = lax.optimization_barrier((mixed_low, *parts))
+    grad_top = jnp.concatenate(parts, 0)
     middle = token_rows + jnp.dot(mixed_low, wo_full, preferred_element_type=f32) + bo
     normed_two, inverse_two = standardize(middle)
     second_in = (normed_two * gain_second + shift_second).astype(bf16)

time: 624 us -> 596 us (0.955)
  waiting for transfers between devices: 240 us -> 219 us
  starting transfers between devices: 47.3 us -> 40.8 us
    ppermute x4 -> x2, waiting for transfers between devices: 83.3 us -> 33.2 us  [to_clip(): lax.ppermute(pick(block[0], (parity + flip) % 2, 0), axes, routes[flip])]
    ppermute x4, waiting for transfers between devices: 20 us -> 41.6 us  [from_clip(): lax.ppermute(rows[flip * slice_len:(flip + 1) * slice_len], axes, back_ro...]
    ppermute x15, starting transfers between devices: 17.1 us -> 9.61 us  [scatter_sum(): lax.ppermute(pick(total, 1 - mine, 1).astype(bf16), 'grp', [(i, i ^ bit)...]
    ppermute x4, starting transfers between devices: 5.62 us -> 12.3 us  [from_clip(): lax.ppermute(rows[flip * slice_len:(flip + 1) * slice_len], axes, back_ro...]
  transfers between devices with their start and end apart: 54 -> 54, of which waited for: 21 -> 23; matrix products, arithmetic and copies ran while one was open for 18% -> 19% of each run, Pallas kernels for 14% -> 7%
where the time goes in v2:
time: 596 us; the launch traced here: 589 us
  waiting for transfers between devices  219 us (37%)
  Pallas kernels  95 us (16%)
  matrix products  92.2 us (15%)
  local copies, waits for them, and re-layouts  86.6 us (15%)
  starting transfers between devices  40.8 us (7%)
  other arithmetic  38 us (6%)
  between operations  17.1 us (3%)
    all_gather x1, waiting for transfers between devices, body(): lax.all_gather(jnp.concatenate([w_query, w_key, w_value, vectors], 1), ax...  59.4 us
    ppermute x15, waiting for transfers between devices, scatter_sum(): lax.ppermute(pick(total, 1 - mine, 1).astype(bf16), 'grp', [(i, i ^ bit)...  56.1 us
    pallas_call x6, Pallas kernels, attend_back(): pl.pallas_call(attend_back_kernel, grid=(count, rows // Q_BLOCK), in_spec...  53.5 us
    ppermute x4, waiting for transfers between devices, from_clip(): lax.ppermute(rows[flip * slice_len:(flip + 1) * slice_len], axes, back_ro...  41.6 us
    pallas_call x1, Pallas kernels, attend(): pl.pallas_call(attend_kernel, grid=(pairs, rows // Q_BLOCK), in_specs=att...  41.5 us
    ppermute x2, waiting for transfers between devices, to_clip(): lax.ppermute(pick(block[0], (parity + flip) % 2, 0), axes, routes[flip])  33.2 us
    dot_general x1, matrix products, body(): hidden = jnp.dot(second_in, up_full, preferred_element_type=f32) + bu  28.6 us
    ppermute x15, waiting for transfers between devices, scatter_sum(): lax.ppermute(pick(total, (seq + offset) % seq_size, 0).astype(bf16), 'seq...  18.8 us
  transfers between devices with their start and end apart: 54, of which 23 were waited for; matrix products, arithmetic and copies ran while one was open for 19% of the time, Pallas kernels for 7%

profile of v2, /device:TPU:9, one launch (start us, length us, event | category | flops | bytes accessed | tf_op | source)
XLA Modules:
  0.0 588.5 jit_solution(11023884743572897845)
XLA Ops:
  16.7 1.7 pad_maximum_fusion.1
  18.4 59.4 %all-gather.3.cloned.1.call-done = bf16[768,2432]{1,0:T(8,128)(2,1)} async-done(((bf16[24,2432]{1,0:T(8,128)(2,1)}), bf16[768,2432]{1,0:T(8,128)(2,1)}) %all-gather.3.cloned.1.call-update) | async-done | bytes 3735568 | tf_op jit(solution)/shard_map/all_gather | solution.py:267
  78.3 3.3 collective-permute-start
  82.6 25.6 %collective-permute-done = bf16[384,768]{0,1:T(8,128)(2,1)S(1)} collective-permute-done((bf16[384,768]{0,1:T(8,128)(2,1)S(1)}, bf16[384,768]{0,1:T(8,128)(2,1)S(1)}, u32[]{:S(2)}, u32[]{:S(2)}) %collective-permute-start) | collective-permute-done | bytes 589856 | tf_op jit(solution)/shard_map/ppermute | solution.py:248
  108.2 7.7 %collective-permute-done.1 = bf16[384,768]{0,1:T(8,128)(2,1)S(1)} collective-permute-done((bf16[384,768]{0,1:T(8,128)(2,1)S(1)}, bf16[384,768]{0,1:T(8,128)(2,1)S(1)}, u32[]{:S(2)}, u32[]{:S(2)}) %collective-permute-start.1) | collective-permute-done | bytes 589856 | tf_op jit(solution)/shard_map/ppermute | solution.py:248
  117.6 1.6 slice_reduce_fusion
  119.3 4.3 add_convert_fusion.q_ref.ko_ref.vo_ref
  123.6 1.6 slice.146
  125.8 4.4 collective-permute-done.3
  132.7 1.9 slice_bitcast_fusion
  134.6 1.8 add.440
  136.4 2.3 constant_dynamic-slice_fusion.4
  138.8 2.3 copy.181
  141.1 2.1 collective-permute-start.4
  143.2 2.1 copy.182
  146.5 41.5 %shard_map.305 = (bf16[768,768]{1,0:T(8,128)(2,1)S(1)}, f32[6,8,768]{2,1,0:T(8,128)S(1)}) custom-call(bf16[768,2304]{1,0:T(8,128)(2,1)S(1)} %add_convert_fusion.q_ref.ko_ref.vo_ref, bf16[768,2304]{1,0:T(8,128)(2,1)S(1)} %add_convert_fusion.q_ref.ko_ref.vo_ref, bf16[768,1536]{1,0:T(8,128)(2,1)} %collective-permute-done.2.kx_ref.vx_ref, ...), custom_call_target="tpu_custom_call" | custom-call | flops 14495514624 | bytes 8257536 | tf_op jit(solution)/shard_map/pallas_call | solution.py:144
  189.6 4.9 collective-permute-done.5
  194.5 1.9 constant_dynamic-update-slice_fusion.1
  197.3 3.2 fusion.112
  202.3 4.8 slice.153
  207.1 8.5 %reshape.221 = bf16[3072,768]{1,0:T(8,128)(2,1)} reshape(bf16[768,3072]{1,0:T(8,128)(2,1)} %slice.153) | data formatting | bytes 9437184 | tf_op jit(solution)/shard_map/reshape | solution.py:281
  215.5 28.6 %fusion.2 = (bf16[768,3072]{1,0:T(8,128)(2,1)}, f32[768,3072]{1,0:T(8,128)S(1)}) fusion(f32[3072]{0:T(1024)} %add.440, bf16[768,6912]{1,0:T(8,128)(2,1)} %all-gather.5.cloned.1.call-done, f32[768,768]{0,1:T(8,128)} %copy-done.45, f32[768]{0:T(1024)S(1)} %get-tuple-element.204, f32[768]{0:T(1024)S(1)} %get-tuple-element.205, f32[768]{0:T(1024)S(1)} %add_rsqrt_fusion, ...), kind=kOutput, calls=%fused_computation.4 | convolution fusion | flops 3782541312 | bytes 21258240 | tf_op jit(solution)/shard_map/dot_general | solution.py:308
  244.2 9.7 %convert_reduce_fusion = (f32[3072]{0:T(1024)}, bf16[768,3072]{1,0:T(8,128)(2,1)S(1)}) fusion(f32[768,3072]{1,0:T(8,128)S(1)} %get-tuple-element.259, f32[3072]{0:T(1024)S(1)} %copy-done.71, bf16[768,768]{0,1:T(8,128)(2,1)} %constant_dynamic-update-slice_fusion, bf16[3072,768]{1,0:T(8,128)(2,1)S(1)} %copy-done.55), kind=kOutput, calls=%fused_computation.11 | convolution fusion | flops 3654546432 | bytes 20078592 | tf_op jit(solution)/shard_map/dot_general | solution.py:316
  253.9 9.9 %fusion.114 = (f32[768]{0:T(1024)}, f32[768,768]{1,0:T(8,128)}) fusion(bf16[768,3072]{1,0:T(8,128)(2,1)S(1)} %get-tuple-element.265, bf16[768,6912]{1,0:T(8,128)(2,1)} %all-gather.5.cloned.1.call-done), kind=kOutput, calls=%fused_computation.253 | convolution fusion | flops 3624467712 | bytes 11799552 | tf_op jit(solution)/shard_map/dot_general | solution.py:320
  263.8 3.1 copy.184
  266.9 3.3 multiply_reduce_fusion
  270.7 2.6 convert_reduce_fusion.4
  273.3 3.3 convolution_convert_fusion.grad_ref
  276.7 8.3 %shard_map.311 = (bf16[768,128]{1,0:T(8,128)(2,1)S(1)}, bf16[768,128]{1,0:T(8,128)(2,1)S(1)}, bf16[768,128]{1,0:T(8,128)(2,1)S(1)}, bf16[768,128]{1,0:T(8,128)(2,1)S(1)}, bf16[768,128]{1,0:T(8,128)(2,1)S(1)}) custom-call(bf16[768,2304]{1,0:T(8,128)(2,1)S(1)} %add_convert_fusion.q_ref.ko_ref.vo_ref, ...), custom_call_target="tpu_custom_call" | custom-call | flops 6039797760 | bytes 2359296 | tf_op jit(solution)/shard_map/pallas_call | solution.py:169
  287.0 9.1 %shard_map.310 = (bf16[768,128]{1,0:T(8,128)(2,1)S(1)}, bf16[768,128]{1,0:T(8,128)(2,1)S(1)}, bf16[768,128]{1,0:T(8,128)(2,1)S(1)}, bf16[768,128]{1,0:T(8,128)(2,1)}, bf16[768,128]{1,0:T(8,128)(2,1)S(1)}) custom-call(bf16[768,2304]{1,0:T(8,128)(2,1)S(1)} %add_convert_fusion.q_ref.ko_ref.vo_ref, bf16[768,2304]{1,0:T(8,128)(2,1)S(1)} %add_convert_fusion.q_ref.ko_ref.vo_ref, ...), custom_call_target="tpu_custom_call" | custom-call | flops 6039797760 | bytes 2359296 | tf_op jit(solution)/shard_map/pallas_call | solution.py:169
  298.1 8.9 %shard_map.309 = (bf16[768,128]{1,0:T(8,128)(2,1)S(1)}, bf16[768,128]{1,0:T(8,128)(2,1)S(1)}, bf16[768,128]{1,0:T(8,128)(2,1)S(1)}, bf16[768,128]{1,0:T(8,128)(2,1)}, bf16[768,128]{1,0:T(8,128)(2,1)S(1)}) custom-call(bf16[768,2304]{1,0:T(8,128)(2,1)S(1)} %add_convert_fusion.q_ref.ko_ref.vo_ref, bf16[768,2304]{1,0:T(8,128)(2,1)S(1)} %add_convert_fusion.q_ref.ko_ref.vo_ref, ...), custom_call_target="tpu_custom_call" | custom-call | flops 6039797760 | bytes 2359296 | tf_op jit(solution)/shard_map/pallas_call | solution.py:169
  308.3 8.9 %shard_map.308 = (bf16[768,128]{1,0:T(8,128)(2,1)S(1)}, bf16[768,128]{1,0:T(8,128)(2,1)S(1)}, bf16[768,128]{1,0:T(8,128)(2,1)S(1)}, bf16[768,128]{1,0:T(8,128)(2,1)}, bf16[768,128]{1,0:T(8,128)(2,1)S(1)}) custom-call(bf16[768,2304]{1,0:T(8,128)(2,1)S(1)} %add_convert_fusion.q_ref.ko_ref.vo_ref, bf16[768,2304]{1,0:T(8,128)(2,1)S(1)} %add_convert_fusion.q_ref.ko_ref.vo_ref, ...), custom_call_target="tpu_custom_call" | custom-call | flops 6039797760 | bytes 2359296 | tf_op jit(solution)/shard_map/pallas_call | solution.py:169
  318.6 9.0 %shard_map.307 = (bf16[768,128]{1,0:T(8,128)(2,1)S(1)}, bf16[768,128]{1,0:T(8,128)(2,1)S(1)}, bf16[768,128]{1,0:T(8,128)(2,1)S(1)}, bf16[768,128]{1,0:T(8,128)(2,1)}, bf16[768,128]{1,0:T(8,128)(2,1)S(1)}) custom-call(bf16[768,2304]{1,0:T(8,128)(2,1)S(1)} %add_convert_fusion.q_ref.ko_ref.vo_ref, bf16[768,2304]{1,0:T(8,128)(2,1)S(1)} %add_convert_fusion.q_ref.ko_ref.vo_ref, ...), custom_call_target="tpu_custom_call" | custom-call | flops 6039797760 | bytes 2359296 | tf_op jit(solution)/shard_map/pallas_call | solution.py:169
  329.0 9.4 %shard_map.306 = (bf16[768,128]{1,0:T(8,128)(2,1)S(1)}, bf16[768,128]{1,0:T(8,128)(2,1)S(1)}, bf16[768,128]{1,0:T(8,128)(2,1)S(1)}, bf16[768,128]{1,0:T(8,128)(2,1)}, bf16[768,128]{1,0:T(8,128)(2,1)S(1)}) custom-call(bf16[768,2304]{1,0:T(8,128)(2,1)S(1)} %add_convert_fusion.q_ref.ko_ref.vo_ref, bf16[768,2304]{1,0:T(8,128)(2,1)S(1)} %add_convert_fusion.q_ref.ko_ref.vo_ref, ...), custom_call_target="tpu_custom_call" | custom-call | flops 6039797760 | bytes 2359296 | tf_op jit(solution)/shard_map/pallas_call | solution.py:169
  338.4 4.0 fusion.106
  344.9 13.4 %fusion.115 = f32[3072,768]{1,0:T(8,128)} fusion(bf16[768,3072]{1,0:T(8,128)(2,1)} %get-tuple-element.258, bf16[768,768]{0,1:T(8,128)(2,1)} %constant_dynamic-update-slice_fusion), kind=kOutput, calls=%fused_computation.254 | convolution fusion | flops 3623878656 | bytes 15335424 | tf_op jit(solution)/shard_map/dot_general | solution.py:314
  358.3 1.8 fusion.39
  361.0 4.5 add_convert_fusion.1
  371.8 4.1 fusion.40
  385.1 5.0 fusion.113
  391.2 2.1 copy.185
  398.5 3.2 concatenate.31
  403.0 5.2 fusion.103
  411.2 1.8 collective-permute-done.47
  418.9 7.2 %collective-permute-start.6 = (bf16[384,768]{0,1:T(8,128)(2,1)}, bf16[384,768]{0,1:T(8,128)(2,1)S(1)}, u32[]{:S(2)}, u32[]{:S(2)}) collective-permute-start(bf16[384,768]{0,1:T(8,128)(2,1)} %get-tuple-element.234), channel_id=1, source_target_pairs={{0,0},{1,1},{4,2},{5,3},{2,4},{3,5},{6,6},{7,7},{8,8},{9,9},{12,10... | collective-permute-start | bytes 1769480 | tf_op jit(solution)/shard_map/ppermute | solution.py:256
  426.2 4.9 collective-permute-start.20
  432.8 1.6 bitcast_add_fusion.6
  435.1 5.2 collective-permute-done.6
  440.3 24.7 %collective-permute-done.7 = bf16[384,768]{0,1:T(8,128)(2,1)S(1)} collective-permute-done((bf16[384,768]{0,1:T(8,128)(2,1)}, bf16[384,768]{0,1:T(8,128)(2,1)S(1)}, u32[]{:S(2)}, u32[]{:S(2)}) %collective-permute-start.7) | collective-permute-done | bytes 589856 | tf_op jit(solution)/shard_map/ppermute | solution.py:256
  465.0 6.2 %collective-permute-done.20 = bf16[384,768]{0,1:T(8,128)(2,1)S(1)} collective-permute-done((bf16[384,768]{0,1:T(8,128)(2,1)}, bf16[384,768]{0,1:T(8,128)(2,1)S(1)}, u32[]{:S(2)}, u32[]{:S(2)}) %collective-permute-start.20) | collective-permute-done | bytes 589856 | tf_op jit(solution)/shard_map/ppermute | solution.py:256
  472.4 5.6 collective-permute-done.21
  478.0 1.6 select_bitcast_fusion.1
  485.1 2.9 bitcast_add_fusion.2
  490.0 3.7 bitcast_add_fusion
  493.9 6.2 %collective-permute-done.23 = bf16[2,96,2304]{2,1,0:T(8,128)(2,1)S(1)} collective-permute-done((bf16[2,96,2304]{2,1,0:T(8,128)(2,1)S(1)}, bf16[2,96,2304]{2,1,0:T(8,128)(2,1)S(1)}, u32[]{:S(2)}, u32[]{:S(2)}) %collective-permute-start.23) | collective-permute-done | bytes 884768 | tf_op jit(solution)/shard_map/ppermute | solution.py:199
  501.7 2.6 bitcast_add_fusion.1
  504.5 6.9 %collective-permute-done.24 = bf16[1,96,2304]{2,1,0:T(8,128)(2,1)S(1)} collective-permute-done((bf16[1,96,2304]{2,1,0:T(8,128)(2,1)S(1)}, bf16[1,96,2304]{2,1,0:T(8,128)(2,1)S(1)}, u32[]{:S(2)}, u32[]{:S(2)}) %collective-permute-start.24) | collective-permute-done | bytes 442400 | tf_op jit(solution)/shard_map/ppermute | solution.py:199
  514.5 2.1 collective-permute-done.25
  517.8 3.0 collective-permute-done.27
  520.8 7.3 %collective-permute-done.41 = bf16[2,384,768]{2,1,0:T(8,128)(2,1)S(1)} collective-permute-done((bf16[2,384,768]{2,1,0:T(8,128)(2,1)S(1)}, bf16[2,384,768]{2,1,0:T(8,128)(2,1)S(1)}, u32[]{:S(2)}, u32[]{:S(2)}) %collective-permute-start.41) | collective-permute-done | bytes 1179680 | tf_op jit(solution)/shard_map/ppermute | solution.py:199
  528.8 22.1 %collective-permute-done.35 = bf16[2,96,3072]{2,1,0:T(8,128)(2,1)S(1)} collective-permute-done((bf16[2,96,3072]{2,1,0:T(8,128)(2,1)S(1)}, bf16[2,96,3072]{2,1,0:T(8,128)(2,1)S(1)}, u32[]{:S(2)}, u32[]{:S(2)}) %collective-permute-start.35) | collective-permute-done | bytes 1179680 | tf_op jit(solution)/shard_map/ppermute | solution.py:199
  554.6 11.1 %collective-permute-done.36 = bf16[1,96,3072]{2,1,0:T(8,128)(2,1)S(1)} collective-permute-done((bf16[1,96,3072]{2,1,0:T(8,128)(2,1)S(1)}, bf16[1,96,3072]{2,1,0:T(8,128)(2,1)S(1)}, u32[]{:S(2)}, u32[]{:S(2)}) %collective-permute-start.36) | collective-permute-done | bytes 589856 | tf_op jit(solution)/shard_map/ppermute | solution.py:199
  567.4 5.6 collective-permute-done.45
  573.8 5.3 collective-permute-done.38
  (378 shorter events, 89.7 us)
Async XLA Ops:
  7.2 70.7 %copy-start.59 = (bf16[1,2,384,768]{3,2,1,0:T(8,128)(2,1)S(1)}, bf16[1,2,384,768]{3,2,1,0:T(8,128)(2,1)}, u32[]{:S(2)}) copy-start(bf16[1,2,384,768]{3,2,1,0:T(8,128)(2,1)} %param.18) | copy-start | bytes 3538948
  7.2 70.6 %all-gather.3.cloned.1.call-start = ((), (), s32[]{:S(2)}) async-start(), calls=%async_computation | async-start | bytes 3852288 | tf_op jit(solution)/shard_map/all_gather | solution.py:267
  15.7 181.7 %all-gather.5.cloned.1.call-start = ((), (), s32[]{:S(2)}) async-start(), calls=%async_computation.1 | async-start | bytes 10948608 | tf_op jit(solution)/shard_map/all_gather | solution.py:272
  78.3 29.9 %collective-permute-start = (bf16[384,768]{0,1:T(8,128)(2,1)S(1)}, bf16[384,768]{0,1:T(8,128)(2,1)S(1)}, u32[]{:S(2)}, u32[]{:S(2)}) collective-permute-start(bf16[384,768]{0,1:T(8,128)(2,1)S(1)} %bitcast.213), channel_id=1, source_target_pairs={{0,0},{1,1},{2,4},{3,5},{4,2},{5,3},{6,6},{7,7},{8,8},{9,9},{10,12... | collective-permute-start | bytes 1769480 | tf_op jit(solution)/shard_map/ppermute | solution.py:248
  81.9 33.9 %collective-permute-start.1 = (bf16[384,768]{0,1:T(8,128)(2,1)S(1)}, bf16[384,768]{0,1:T(8,128)(2,1)S(1)}, u32[]{:S(2)}, u32[]{:S(2)}) collective-permute-start(bf16[384,768]{0,1:T(8,128)(2,1)S(1)} %bitcast.214), channel_id=1, source_target_pairs={{0,1},{1,0},{2,5},{3,4},{4,3},{5,2},{6,7},{7,6},{8,9},{9,8},{10,13... | collective-permute-start | bytes 1769480 | tf_op jit(solution)/shard_map/ppermute | solution.py:248
  125.3 11.2 %collective-permute-start.2 = (bf16[768,1536]{1,0:T(8,128)(2,1)}, bf16[768,1536]{1,0:T(8,128)(2,1)}, u32[]{:S(2)}, u32[]{:S(2)}) collective-permute-start(bf16[768,1536]{1,0:T(8,128)(2,1)} %slice.146), channel_id=1, source_target_pairs={{0,4},{4,0},{8,12},{12,8},{16,20},{20,16},{24,28},{28,24},{1,5},{5... | collective-permute-start | bytes 7077896 | tf_op jit(solution)/shard_map/ppermute | solution.py:296
  125.3 4.9 collective-permute-start.3
  141.1 48.6 %collective-permute-start.4 = (bf16[384,768]{0,1:T(8,128)(2,1)}, bf16[384,768]{0,1:T(8,128)(2,1)}, u32[]{:S(2)}, u32[]{:S(2)}) collective-permute-start(bf16[384,768]{0,1:T(8,128)(2,1)} %bitcast.211), channel_id=1, source_target_pairs={{0,0},{1,1},{2,4},{3,5},{4,2},{5,3},{6,6},{7,7},{8,8},{9,9},{10,12... | collective-permute-start | bytes 1769480 | tf_op jit(solution)/shard_map/ppermute | solution.py:299
  145.3 49.2 %collective-permute-start.5 = (bf16[384,768]{0,1:T(8,128)(2,1)}, bf16[384,768]{0,1:T(8,128)(2,1)S(1)}, u32[]{:S(2)}, u32[]{:S(2)}) collective-permute-start(bf16[384,768]{0,1:T(8,128)(2,1)} %bitcast.212), channel_id=1, source_target_pairs={{0,1},{1,0},{2,5},{3,4},{4,3},{5,2},{6,7},{7,6},{8,9},{9,8},{10,13... | collective-permute-start | bytes 1769480 | tf_op jit(solution)/shard_map/ppermute | solution.py:299
  146.4 41.5 %copy-start = (f32[768,256]{1,0:T(8,128)}, f32[768,256]{1,0:T(8,128)S(1)}, u32[]{:S(2)}) copy-start(f32[768,256]{1,0:T(8,128)S(1)} %broadcast_in_dim.16.bias_ref) | copy-start | bytes 2359300
  215.5 28.7 %copy-start.55 = (bf16[3072,768]{1,0:T(8,128)(2,1)S(1)}, bf16[3072,768]{1,0:T(8,128)(2,1)}, u32[]{:S(2)}) copy-start(bf16[3072,768]{1,0:T(8,128)(2,1)} %reshape.221) | copy-start | bytes 14155780
  215.5 28.7 %copy-start.71 = (f32[3072]{0:T(1024)S(1)}, f32[3072]{0:T(1024)}, u32[]{:S(2)}) copy-start(f32[3072]{0:T(1024)} %add.440) | copy-start | bytes 36868
  273.3 69.1 %copy-start.52 = (f32[768,768]{0,1:T(8,128)}, f32[768,768]{0,1:T(8,128)S(1)}, u32[]{:S(2)}) copy-start(f32[768,768]{0,1:T(8,128)S(1)} %get-tuple-element.220) | copy-start | bytes 7077892
  318.6 19.8 %slice-start.5 = ((s8[4718592]{0:T(1024)(128)(4,1)}), s8[4194304]{0:T(1024)(128)(4,1)S(1)}, s32[]{:S(2)}) async-start(s8[4718592]{0:T(1024)(128)(4,1)} %bitcast.225), calls=%async_computation.7 | async-start | bytes 8388608
  342.5 18.5 %slice-start.3 = ((s8[4718592]{0:T(1024)(128)(4,1)}), s8[524288]{0:T(1024)(128)(4,1)S(1)}, s32[]{:S(2)}) async-start(s8[4718592]{0:T(1024)(128)(4,1)} %bitcast.190), calls=%async_computation.5 | async-start | bytes 1048576
  342.5 18.5 %slice-start.7 = ((s8[4718592]{0:T(1024)(128)(4,1)}), s8[4194304]{0:T(1024)(128)(4,1)S(1)}, s32[]{:S(2)}) async-start(s8[4718592]{0:T(1024)(128)(4,1)} %bitcast.227), calls=%async_computation.9 | async-start | bytes 8388608
  343.6 16.4 %copy-start.58 = (f32[768,768]{1,0:T(8,128)}, f32[768,768]{1,0:T(8,128)S(1)}, u32[]{:S(2)}) copy-start(f32[768,768]{1,0:T(8,128)S(1)} %fusion.100) | copy-start | bytes 7077892
  343.7 32.3 %collective-permute-start.8 = (bf16[768,128]{1,0:T(8,128)(2,1)}, bf16[768,128]{1,0:T(8,128)(2,1)}, u32[]{:S(2)}, u32[]{:S(2)}) collective-permute-start(bf16[768,128]{1,0:T(8,128)(2,1)} %get-tuple-element.72), channel_id=1, source_target_pairs={{0,4},{4,0},{8,12},{12,8},{16,20},{20,16},{24,28},{28,24},{1,5},{5... | collective-permute-start | bytes 589832 | tf_op jit(solution)/shard_map/ppermute | solution.py:343
  343.8 33.5 %collective-permute-start.9 = (bf16[768,128]{1,0:T(8,128)(2,1)}, bf16[768,128]{1,0:T(8,128)(2,1)}, u32[]{:S(2)}, u32[]{:S(2)}) collective-permute-start(bf16[768,128]{1,0:T(8,128)(2,1)} %get-tuple-element.74), channel_id=1, source_target_pairs={{0,4},{4,0},{8,12},{12,8},{16,20},{20,16},{24,28},{28,24},{1,5},{5... | collective-permute-start | bytes 589832 | tf_op jit(solution)/shard_map/ppermute | solution.py:343
  344.3 34.5 %collective-permute-start.10 = (bf16[768,128]{1,0:T(8,128)(2,1)}, bf16[768,128]{1,0:T(8,128)(2,1)}, u32[]{:S(2)}, u32[]{:S(2)}) collective-permute-start(bf16[768,128]{1,0:T(8,128)(2,1)} %get-tuple-element.76), channel_id=1, source_target_pairs={{0,4},{4,0},{8,12},{12,8},{16,20},{20,16},{24,28},{28,24},{1,5},{5... | collective-permute-start | bytes 589832 | tf_op jit(solution)/shard_map/ppermute | solution.py:343
  344.4 35.7 %collective-permute-start.11 = (bf16[768,128]{1,0:T(8,128)(2,1)}, bf16[768,128]{1,0:T(8,128)(2,1)}, u32[]{:S(2)}, u32[]{:S(2)}) collective-permute-start(bf16[768,128]{1,0:T(8,128)(2,1)} %get-tuple-element.78), channel_id=1, source_target_pairs={{0,4},{4,0},{8,12},{12,8},{16,20},{20,16},{24,28},{28,24},{1,5},{5... | collective-permute-start | bytes 589832 | tf_op jit(solution)/shard_map/ppermute | solution.py:343
  344.8 36.8 %collective-permute-start.12 = (bf16[768,128]{1,0:T(8,128)(2,1)}, bf16[768,128]{1,0:T(8,128)(2,1)}, u32[]{:S(2)}, u32[]{:S(2)}) collective-permute-start(bf16[768,128]{1,0:T(8,128)(2,1)} %get-tuple-element.80), channel_id=1, source_target_pairs={{0,4},{4,0},{8,12},{12,8},{16,20},{20,16},{24,28},{28,24},{1,5},{5... | collective-permute-start | bytes 589832 | tf_op jit(solution)/shard_map/ppermute | solution.py:343
  344.9 16.1 %slice-start.8 = ((s8[4718592]{0:T(1024)(128)(4,1)}), s8[524288]{0:T(1024)(128)(4,1)S(1)}, s32[]{:S(2)}) async-start(s8[4718592]{0:T(1024)(128)(4,1)} %bitcast.227), calls=%async_computation.10 | async-start | bytes 1048576
  376.0 7.0 %collective-permute-start.13 = (bf16[768,128]{1,0:T(8,128)(2,1)S(1)}, bf16[768,128]{1,0:T(8,128)(2,1)S(1)}, u32[]{:S(2)}, u32[]{:S(2)}) collective-permute-start(bf16[768,128]{1,0:T(8,128)(2,1)S(1)} %copy-done.35), channel_id=1, source_target_pairs={{0,4},{4,0},{8,12},{12,8},{16,20},{20,16},{24,28},{28,24},{1,5},{5... | collective-permute-start | bytes 589832 | tf_op jit(solution)/shard_map/ppermute | solution.py:343
  377.3 6.2 %collective-permute-start.14 = (bf16[768,128]{1,0:T(8,128)(2,1)S(1)}, bf16[768,128]{1,0:T(8,128)(2,1)S(1)}, u32[]{:S(2)}, u32[]{:S(2)}) collective-permute-start(bf16[768,128]{1,0:T(8,128)(2,1)S(1)} %copy-done.39), channel_id=1, source_target_pairs={{0,4},{4,0},{8,12},{12,8},{16,20},{20,16},{24,28},{28,24},{1,5},{5... | collective-permute-start | bytes 589832 | tf_op jit(solution)/shard_map/ppermute | solution.py:343
  378.8 5.0 collective-permute-start.15
  380.1 4.2 collective-permute-start.16
  381.6 2.8 collective-permute-start.17
  383.0 1.5 collective-permute-start.18
  383.5 1.5 collective-permute-start.19
  383.8 47.4 %collective-permute-start.28 = (bf16[4,96,768]{2,1,0:T(8,128)(2,1)}, bf16[4,96,768]{2,1,0:T(8,128)(2,1)}, u32[]{:S(2)}, u32[]{:S(2)}) collective-permute-start(bf16[4,96,768]{2,1,0:T(8,128)(2,1)} %fusion.47), channel_id=1, source_target_pairs={{0,4},{4,0},{8,12},{12,8},{16,20},{20,16},{24,28},{28,24},{1,5},{5... | collective-permute-start | bytes 1769480 | tf_op jit(solution)/shard_map/ppermute | solution.py:199
  402.7 7.2 %collective-permute-start.46 = (bf16[4,96,128]{2,1,0:T(8,128)(2,1)S(1)}, bf16[4,96,128]{2,1,0:T(8,128)(2,1)S(1)}, u32[]{:S(2)}, u32[]{:S(2)}) collective-permute-start(bf16[4,96,128]{2,1,0:T(8,128)(2,1)S(1)} %fusion.78), channel_id=1, source_target_pairs={{0,4},{4,0},{8,12},{12,8},{16,20},{20,16},{24,28},{28,24},{1,5},{5... | collective-permute-start | bytes 294920 | tf_op jit(solution)/shard_map/ppermute | solution.py:199
  409.6 75.5 %collective-permute-start.22 = (bf16[4,96,2304]{2,1,0:T(8,128)(2,1)}, bf16[4,96,2304]{2,1,0:T(8,128)(2,1)}, u32[]{:S(2)}, u32[]{:S(2)}) collective-permute-start(bf16[4,96,2304]{2,1,0:T(8,128)(2,1)} %fusion.41), channel_id=1, source_target_pairs={{0,4},{4,0},{8,12},{12,8},{16,20},{20,16},{24,28},{28,24},{1,5},{5... | collective-permute-start | bytes 5308424 | tf_op jit(solution)/shard_map/ppermute | solution.py:199
  410.0 3.0 collective-permute-start.47
  413.0 2.7 collective-permute-start.48
  415.8 3.1 collective-permute-start.49
  416.5 9.6 %collective-permute-start.50 = (bf16[24,128]{1,0:T(8,128)(2,1)S(1)}, bf16[24,128]{1,0:T(8,128)(2,1)S(1)}, u32[]{:S(2)}, u32[]{:S(2)}) collective-permute-start(bf16[24,128]{1,0:T(8,128)(2,1)S(1)} %get-tuple-element.251), channel_id=1, source_target_pairs={{0,2},{1,3},{2,0},{3,1},{4,6},{5,7},{6,4},{7,5},{8,10},{9,11},{10,... | collective-permute-start | bytes 18440 | tf_op jit(solution)/shard_map/ppermute | solution.py:207
  417.8 8.4 %collective-permute-start.51 = (bf16[24,128]{1,0:T(8,128)(2,1)S(1)}, bf16[24,128]{1,0:T(8,128)(2,1)S(1)}, u32[]{:S(2)}, u32[]{:S(2)}) collective-permute-start(bf16[24,128]{1,0:T(8,128)(2,1)S(1)} %get-tuple-element.250), channel_id=1, source_target_pairs={{0,3},{1,0},{2,1},{3,2},{4,7},{5,4},{6,5},{7,6},{8,11},{9,8},{10,9... | collective-permute-start | bytes 18440 | tf_op jit(solution)/shard_map/ppermute | solution.py:207
  418.9 21.4 %collective-permute-start.6 = (bf16[384,768]{0,1:T(8,128)(2,1)}, bf16[384,768]{0,1:T(8,128)(2,1)S(1)}, u32[]{:S(2)}, u32[]{:S(2)}) collective-permute-start(bf16[384,768]{0,1:T(8,128)(2,1)} %get-tuple-element.234), channel_id=1, source_target_pairs={{0,0},{1,1},{4,2},{5,3},{2,4},{3,5},{6,6},{7,7},{8,8},{9,9},{12,10... | collective-permute-start | bytes 1769480 | tf_op jit(solution)/shard_map/ppermute | solution.py:256
  426.2 38.9 %collective-permute-start.7 = (bf16[384,768]{0,1:T(8,128)(2,1)}, bf16[384,768]{0,1:T(8,128)(2,1)S(1)}, u32[]{:S(2)}, u32[]{:S(2)}) collective-permute-start(bf16[384,768]{0,1:T(8,128)(2,1)} %get-tuple-element.235), channel_id=1, source_target_pairs={{1,0},{0,1},{5,2},{4,3},{3,4},{2,5},{7,6},{6,7},{9,8},{8,9},{13,10... | collective-permute-start | bytes 1769480 | tf_op jit(solution)/shard_map/ppermute | solution.py:256
  426.2 44.9 %collective-permute-start.20 = (bf16[384,768]{0,1:T(8,128)(2,1)}, bf16[384,768]{0,1:T(8,128)(2,1)S(1)}, u32[]{:S(2)}, u32[]{:S(2)}) collective-permute-start(bf16[384,768]{0,1:T(8,128)(2,1)} %get-tuple-element.230), channel_id=1, source_target_pairs={{0,0},{1,1},{4,2},{5,3},{2,4},{3,5},{6,6},{7,7},{8,8},{9,9},{12,10... | collective-permute-start | bytes 1769480 | tf_op jit(solution)/shard_map/ppermute | solution.py:256
  431.2 46.8 %collective-permute-start.21 = (bf16[384,768]{0,1:T(8,128)(2,1)}, bf16[384,768]{0,1:T(8,128)(2,1)}, u32[]{:S(2)}, u32[]{:S(2)}) collective-permute-start(bf16[384,768]{0,1:T(8,128)(2,1)} %get-tuple-element.231), channel_id=1, source_target_pairs={{1,0},{0,1},{5,2},{4,3},{3,4},{2,5},{7,6},{6,7},{9,8},{8,9},{13,10... | collective-permute-start | bytes 1769480 | tf_op jit(solution)/shard_map/ppermute | solution.py:256
  440.3 49.4 %collective-permute-start.40 = (bf16[4,384,768]{2,1,0:T(8,128)(2,1)}, bf16[4,384,768]{2,1,0:T(8,128)(2,1)}, u32[]{:S(2)}, u32[]{:S(2)}) collective-permute-start(bf16[4,384,768]{2,1,0:T(8,128)(2,1)} %fusion.40), channel_id=1, source_target_pairs={{0,4},{4,0},{8,12},{12,8},{16,20},{20,16},{24,28},{28,24},{1,5},{5... | collective-permute-start | bytes 7077896 | tf_op jit(solution)/shard_map/ppermute | solution.py:199
  465.0 35.5 %collective-permute-start.34 = (bf16[4,96,3072]{2,1,0:T(8,128)(2,1)}, bf16[4,96,3072]{2,1,0:T(8,128)(2,1)}, u32[]{:S(2)}, u32[]{:S(2)}) collective-permute-start(bf16[4,96,3072]{2,1,0:T(8,128)(2,1)} %fusion.39), channel_id=1, source_target_pairs={{0,4},{4,0},{8,12},{12,8},{16,20},{20,16},{24,28},{28,24},{1,5},{5... | collective-permute-start | bytes 7077896 | tf_op jit(solution)/shard_map/ppermute | solution.py:199
  471.2 11.6 %collective-permute-start.29 = (bf16[2,96,768]{2,1,0:T(8,128)(2,1)}, bf16[2,96,768]{2,1,0:T(8,128)(2,1)}, u32[]{:S(2)}, u32[]{:S(2)}) collective-permute-start(bf16[2,96,768]{2,1,0:T(8,128)(2,1)} %fusion.48), channel_id=1, source_target_pairs={{0,8},{4,12},{8,0},{12,4},{16,24},{20,28},{24,16},{28,20},{1,9},{5... | collective-permute-start | bytes 884744 | tf_op jit(solution)/shard_map/ppermute | solution.py:199
  483.8 4.6 collective-permute-start.30
  488.1 12.0 %collective-permute-start.23 = (bf16[2,96,2304]{2,1,0:T(8,128)(2,1)S(1)}, bf16[2,96,2304]{2,1,0:T(8,128)(2,1)S(1)}, u32[]{:S(2)}, u32[]{:S(2)}) collective-permute-start(bf16[2,96,2304]{2,1,0:T(8,128)(2,1)S(1)} %fusion.46), channel_id=1, source_target_pairs={{0,8},{4,12},{8,0},{12,4},{16,24},{20,28},{24,16},{28,20},{1,9},{5... | collective-permute-start | bytes 2654216 | tf_op jit(solution)/shard_map/ppermute | solution.py:199
  488.5 23.8 %collective-permute-start.31 = (bf16[24,768]{1,0:T(8,128)(2,1)S(1)}, bf16[24,768]{1,0:T(8,128)(2,1)S(1)}, u32[]{:S(2)}, u32[]{:S(2)}) collective-permute-start(bf16[24,768]{1,0:T(8,128)(2,1)S(1)} %get-tuple-element.243), channel_id=1, source_target_pairs={{0,1},{1,2},{2,3},{3,0},{4,5},{5,6},{6,7},{7,4},{8,9},{9,10},{10,1... | collective-permute-start | bytes 110600 | tf_op jit(solution)/shard_map/ppermute | solution.py:207
  488.6 23.8 %collective-permute-start.32 = (bf16[24,768]{1,0:T(8,128)(2,1)S(1)}, bf16[24,768]{1,0:T(8,128)(2,1)S(1)}, u32[]{:S(2)}, u32[]{:S(2)}) collective-permute-start(bf16[24,768]{1,0:T(8,128)(2,1)S(1)} %get-tuple-element.245), channel_id=1, source_target_pairs={{0,2},{1,3},{2,0},{3,1},{4,6},{5,7},{6,4},{7,5},{8,10},{9,11},{10,... | collective-permute-start | bytes 110600 | tf_op jit(solution)/shard_map/ppermute | solution.py:207
  489.7 22.8 %collective-permute-start.33 = (bf16[24,768]{1,0:T(8,128)(2,1)S(1)}, bf16[24,768]{1,0:T(8,128)(2,1)S(1)}, u32[]{:S(2)}, u32[]{:S(2)}) collective-permute-start(bf16[24,768]{1,0:T(8,128)(2,1)S(1)} %get-tuple-element.244), channel_id=1, source_target_pairs={{0,3},{1,0},{2,1},{3,2},{4,7},{5,4},{6,5},{7,6},{8,11},{9,8},{10,9... | collective-permute-start | bytes 110600 | tf_op jit(solution)/shard_map/ppermute | solution.py:207
  500.1 28.1 %collective-permute-start.41 = (bf16[2,384,768]{2,1,0:T(8,128)(2,1)S(1)}, bf16[2,384,768]{2,1,0:T(8,128)(2,1)S(1)}, u32[]{:S(2)}, u32[]{:S(2)}) collective-permute-start(bf16[2,384,768]{2,1,0:T(8,128)(2,1)S(1)} %fusion.43), channel_id=1, source_target_pairs={{0,8},{4,12},{8,0},{12,4},{16,24},{20,28},{24,16},{28,20},{1,9},{5... | collective-permute-start | bytes 3538952 | tf_op jit(solution)/shard_map/ppermute | solution.py:199
  500.6 10.9 %collective-permute-start.24 = (bf16[1,96,2304]{2,1,0:T(8,128)(2,1)S(1)}, bf16[1,96,2304]{2,1,0:T(8,128)(2,1)S(1)}, u32[]{:S(2)}, u32[]{:S(2)}) collective-permute-start(bf16[1,96,2304]{2,1,0:T(8,128)(2,1)S(1)} %dynamic-slice_convert_fusion.6), channel_id=1, source_target_pairs={{0,16},{4,20},{8,24},{12,28},{16,0},{20,4},{24,8},{28,12},{1,17},{... | collective-permute-start | bytes 1327112 | tf_op jit(solution)/shard_map/ppermute | solution.py:199
  511.4 39.5 %collective-permute-start.35 = (bf16[2,96,3072]{2,1,0:T(8,128)(2,1)S(1)}, bf16[2,96,3072]{2,1,0:T(8,128)(2,1)S(1)}, u32[]{:S(2)}, u32[]{:S(2)}) collective-permute-start(bf16[2,96,3072]{2,1,0:T(8,128)(2,1)S(1)} %fusion.42), channel_id=1, source_target_pairs={{0,8},{4,12},{8,0},{12,4},{16,24},{20,28},{24,16},{28,20},{1,9},{5... | collective-permute-start | bytes 3538952 | tf_op jit(solution)/shard_map/ppermute | solution.py:199
  512.3 4.3 collective-permute-start.25
  512.4 5.4 collective-permute-start.26
  512.5 8.3 %collective-permute-start.27 = (bf16[24,2304]{1,0:T(8,128)(2,1)S(1)}, bf16[24,2304]{1,0:T(8,128)(2,1)S(1)}, u32[]{:S(2)}, u32[]{:S(2)}) collective-permute-start(bf16[24,2304]{1,0:T(8,128)(2,1)S(1)} %get-tuple-element.241), channel_id=1, source_target_pairs={{0,3},{1,0},{2,1},{3,2},{4,7},{5,4},{6,5},{7,6},{8,11},{9,8},{10,9... | collective-permute-start | bytes 331784 | tf_op jit(solution)/shard_map/ppermute | solution.py:207
  528.4 24.4 %collective-permute-start.42 = (bf16[1,384,768]{2,1,0:T(8,128)(2,1)S(1)}, bf16[1,384,768]{2,1,0:T(8,128)(2,1)S(1)}, u32[]{:S(2)}, u32[]{:S(2)}) collective-permute-start(bf16[1,384,768]{2,1,0:T(8,128)(2,1)S(1)} %dynamic-slice_convert_fusion.3), channel_id=1, source_target_pairs={{0,16},{4,20},{8,24},{12,28},{16,0},{20,4},{24,8},{28,12},{1,17},{... | collective-permute-start | bytes 1769480 | tf_op jit(solution)/shard_map/ppermute | solution.py:199
  551.3 14.3 %collective-permute-start.36 = (bf16[1,96,3072]{2,1,0:T(8,128)(2,1)S(1)}, bf16[1,96,3072]{2,1,0:T(8,128)(2,1)S(1)}, u32[]{:S(2)}, u32[]{:S(2)}) collective-permute-start(bf16[1,96,3072]{2,1,0:T(8,128)(2,1)S(1)} %dynamic-slice_convert_fusion.4), channel_id=1, source_target_pairs={{0,16},{4,20},{8,24},{12,28},{16,0},{20,4},{24,8},{28,12},{1,17},{... | collective-permute-start | bytes 1769480 | tf_op jit(solution)/shard_map/ppermute | solution.py:199
  553.0 13.0 %collective-permute-start.43 = (bf16[96,768]{1,0:T(8,128)(2,1)S(1)}, bf16[96,768]{1,0:T(8,128)(2,1)S(1)}, u32[]{:S(2)}, u32[]{:S(2)}) collective-permute-start(bf16[96,768]{1,0:T(8,128)(2,1)S(1)} %get-tuple-element.222), channel_id=1, source_target_pairs={{0,1},{1,2},{2,3},{3,0},{4,5},{5,6},{6,7},{7,4},{8,9},{9,10},{10,1... | collective-permute-start | bytes 442376 | tf_op jit(solution)/shard_map/ppermute | solution.py:207
  553.1 14.3 %collective-permute-start.44 = (bf16[96,768]{1,0:T(8,128)(2,1)S(1)}, bf16[96,768]{1,0:T(8,128)(2,1)S(1)}, u32[]{:S(2)}, u32[]{:S(2)}) collective-permute-start(bf16[96,768]{1,0:T(8,128)(2,1)S(1)} %get-tuple-element.224), channel_id=1, source_target_pairs={{0,2},{1,3},{2,0},{3,1},{4,6},{5,7},{6,4},{7,5},{8,10},{9,11},{10,... | collective-permute-start | bytes 442376 | tf_op jit(solution)/shard_map/ppermute | solution.py:207
  554.2 18.8 %collective-permute-start.45 = (bf16[96,768]{1,0:T(8,128)(2,1)S(1)}, bf16[96,768]{1,0:T(8,128)(2,1)S(1)}, u32[]{:S(2)}, u32[]{:S(2)}) collective-permute-start(bf16[96,768]{1,0:T(8,128)(2,1)S(1)} %get-tuple-element.223), channel_id=1, source_target_pairs={{0,3},{1,0},{2,1},{3,2},{4,7},{5,4},{6,5},{7,6},{8,11},{9,8},{10,9... | collective-permute-start | bytes 442376 | tf_op jit(solution)/shard_map/ppermute | solution.py:207
  565.8 7.9 %collective-permute-start.37 = (bf16[24,3072]{1,0:T(8,128)(2,1)S(1)}, bf16[24,3072]{1,0:T(8,128)(2,1)S(1)}, u32[]{:S(2)}, u32[]{:S(2)}) collective-permute-start(bf16[24,3072]{1,0:T(8,128)(2,1)S(1)} %get-tuple-element.225), channel_id=1, source_target_pairs={{0,1},{1,2},{2,3},{3,0},{4,5},{5,6},{6,7},{7,4},{8,9},{9,10},{10,1... | collective-permute-start | bytes 442376 | tf_op jit(solution)/shard_map/ppermute | solution.py:207
  565.9 13.2 %collective-permute-start.38 = (bf16[24,3072]{1,0:T(8,128)(2,1)S(1)}, bf16[24,3072]{1,0:T(8,128)(2,1)S(1)}, u32[]{:S(2)}, u32[]{:S(2)}) collective-permute-start(bf16[24,3072]{1,0:T(8,128)(2,1)S(1)} %get-tuple-element.227), channel_id=1, source_target_pairs={{0,2},{1,3},{2,0},{3,1},{4,6},{5,7},{6,4},{7,5},{8,10},{9,11},{10,... | collective-permute-start | bytes 442376 | tf_op jit(solution)/shard_map/ppermute | solution.py:207
  566.0 14.7 %collective-permute-start.39 = (bf16[24,3072]{1,0:T(8,128)(2,1)S(1)}, bf16[24,3072]{1,0:T(8,128)(2,1)S(1)}, u32[]{:S(2)}, u32[]{:S(2)}) collective-permute-start(bf16[24,3072]{1,0:T(8,128)(2,1)S(1)} %get-tuple-element.226), channel_id=1, source_target_pairs={{0,3},{1,0},{2,1},{3,2},{4,7},{5,4},{6,5},{7,6},{8,11},{9,8},{10,9... | collective-permute-start | bytes 442376 | tf_op jit(solution)/shard_map/ppermute | solution.py:207
  (78 other events, 380.6 us)
Sparse Core Ops, SparseCore 0:
  15.8 61.9 all-gather.2
  80.6 108.7 all-gather.4
